TPU v7x, 512 devices: a whole 4x4x16 slice. The times are simulated.
512 devices in a mesh: dp: 32 (over z_lo, x), sp: 16 (over y, z_hi, core).
Axes of the slice: x: 4, y: 4, z: 16 (z_hi: 2, z_lo: 8; z = z_hi * 8 + z_lo), core: 2. Of those that a mesh axis runs over, the one named last changes fastest.
Arguments:
- query: bfloat16 [4096, 12288], P(('dp', 'sp')), parts along dimension 0, may hold values from -24 to 24
- grad_out: bfloat16 [4096, 8192], P(('dp', 'sp')), parts along dimension 0, may hold values from -6 to 6
- latent: bfloat16 [65536, 512], P(('dp', 'sp')), parts along dimension 0, may hold values from -6 to 6
- rope_key: bfloat16 [65536, 64], P(('dp', 'sp')), parts along dimension 0, may hold values from -6 to 6
- w_key: bfloat16 [512, 8192], P(None, 'sp'), may hold values from -0.5 to 0.5
- w_value: bfloat16 [512, 8192], P(None, 'sp'), may hold values from -0.5 to 0.5
- offset: int32 [32], P('dp'), parts along dimension 0, may hold values from 0 to 1920
Outputs:
- d_query: bfloat16 [4096, 12288], P(('dp', 'sp')), parts along dimension 0
- d_latent: bfloat16 [65536, 512], P(('dp', 'sp')), parts along dimension 0
- d_rope_key: bfloat16 [65536, 64], P(('dp', 'sp')), parts along dimension 0
There are 32 independent parts, one for each index of `dp`. A program takes and returns all parts, laid end to end along the dimension named above; an argument that names none is the same for every part. Nothing has to cross between parts.
All inputs are finite; a program needn't handle non-finite values.
Results may differ from a plain program's by a relative error of at most 0.023.
Values may be sent and summed in bfloat16 or wider, within the bound.
No kernel may reach another device: no remote copies, remote signals or barrier semaphores. Data moves between devices by JAX's collectives and lax.ppermute only.
A program may use at most 64 MiB of HBM per device.

v0:
```python
import jax
import jax.numpy as jnp
from jax import lax
from jax.sharding import PartitionSpec as P

NOPE = 128
ROPE = 64
VDIM = 128
LATENT = 512


def contract(left, right):
    return lax.dot_general(
        left, right, (((1,), (1,)), ((), ())), preferred_element_type=jnp.float32
    )


def inner(left, right):
    return lax.dot_general(
        left, right, (((0,), (0,)), ((), ())), preferred_element_type=jnp.float32
    )


def on_device(query, grad_out, latent, rope_key, w_key, w_value, offset):
    width = NOPE + ROPE
    scale = width ** (-0.5)
    heads = w_key.shape[1] // NOPE
    query_heads, grad_heads = (
        lax.all_to_all(query, "sp", split_axis=1, concat_axis=0, tiled=True),
        lax.all_to_all(grad_out, "sp", split_axis=1, concat_axis=0, tiled=True),
    )
    count = query_heads.shape[0]
    stacked = heads * count
    query3 = query_heads.reshape(count, heads, width)
    key_proj = w_key.reshape(LATENT, heads, NOPE)
    value_proj = w_value.reshape(LATENT, heads, VDIM)
    q_lat = jnp.einsum(
        "qhn,lhn->hql", query3[:, :, :NOPE], key_proj, preferred_element_type=jnp.float32
    )
    q_lat = q_lat.astype(jnp.bfloat16).reshape(stacked, LATENT)
    q_rot = jnp.transpose(query3[:, :, NOPE:], (1, 0, 2)).reshape(stacked, ROPE)
    d_olat = jnp.einsum(
        "qhv,lhv->hql",
        grad_heads.reshape(count, heads, VDIM),
        value_proj,
        preferred_element_type=jnp.float32,
    )
    d_olat = d_olat.astype(jnp.bfloat16).reshape(stacked, LATENT)
    positions = offset[0] + jnp.tile(jnp.arange(count, dtype=jnp.int32), heads)
    lat_full, rot_full = (
        lax.all_gather(latent, "sp", axis=0, tiled=True),
        lax.all_gather(rope_key, "sp", axis=0, tiled=True),
    )
    total = lat_full.shape[0]
    scores = (contract(q_lat, lat_full) + contract(q_rot, rot_full)) * scale
    key_pos = jnp.arange(total, dtype=jnp.int32)
    visible = key_pos[None, :] <= positions[:, None]
    top = jnp.max(jnp.where(visible, scores, -1e30), axis=1, keepdims=True)
    expo = jnp.where(visible, jnp.exp(scores - top), 0.0)
    probs = expo / jnp.sum(expo, axis=1, keepdims=True)
    dprob = contract(d_olat, lat_full)
    delta = jnp.sum(probs * dprob, axis=1, keepdims=True)
    dscore = (probs * (dprob - delta) * scale).astype(jnp.bfloat16)
    probs_low = probs.astype(jnp.bfloat16)
    dq_lat = jnp.dot(dscore, lat_full, preferred_element_type=jnp.float32).astype(jnp.bfloat16)
    dq_rot = jnp.dot(dscore, rot_full, preferred_element_type=jnp.float32).astype(jnp.bfloat16)
    lat_term = inner(dscore, q_lat) + inner(probs_low, d_olat)
    rot_term = inner(dscore, q_rot)
    summed = lax.psum_scatter(
        jnp.concatenate([lat_term, rot_term], axis=1).astype(jnp.bfloat16),
        "sp",
        scatter_dimension=0,
        tiled=True,
    ).astype(jnp.float32)
    dq_plain = jnp.einsum(
        "hql,lhn->qhn",
        dq_lat.reshape(heads, count, LATENT),
        key_proj,
        preferred_element_type=jnp.float32,
    ).astype(jnp.bfloat16)
    dq_rot3 = jnp.transpose(dq_rot.reshape(heads, count, ROPE), (1, 0, 2))
    d_heads = jnp.concatenate([dq_plain, dq_rot3], axis=2).reshape(count, heads * width)
    d_query = lax.all_to_all(d_heads, "sp", split_axis=0, concat_axis=1, tiled=True)
    d_latent = summed[:, :LATENT].astype(jnp.bfloat16)
    d_rope_key = summed[:, LATENT:].astype(jnp.bfloat16)
    return (d_query, d_latent, d_rope_key)


def solution(mesh):
    placed = (
        P(("dp", "sp"), None),
        P(("dp", "sp"), None),
        P(("dp", "sp"), None),
        P(("dp", "sp"), None),
        P(None, "sp"),
        P(None, "sp"),
        P("dp"),
    )
    return jax.shard_map(
        on_device,
        mesh=mesh,
        in_specs=placed,
        out_specs=(P(("dp", "sp"), None), P(("dp", "sp"), None), P(("dp", "sp"), None)),
        check_vma=False,
    )
```

profile of v0, /device:TPU:4, one launch (start us, length us, event | category | flops | bytes accessed | tf_op | source)
XLA Modules:
  0.0 267.7 jit_solution(7322056509379048348)
XLA Ops:
  7.2 0.0 copy-start
  7.2 0.0 all-gather.2.cloned.1.call-start
  7.2 0.7 all-gather.2.cloned.1.call-update
  7.9 33.4 %all_to_all.51 = bf16[8,16,512]{2,0,1:T(8,128)(2,1)S(1)} all-to-all(bf16[8,16,512]{2,0,1:T(8,128)(2,1)} %bitcast.75), channel_id=1, replica_groups=mesh['dp'=32,'sp'=16] {'sp'}, dimensions={1} | all-to-all | bytes 262144 | tf_op jit(solution)/shard_map/all_to_all | solution.py:30
  41.3 3.5 %all-to-all-start = ((bf16[8,16,768]{2,0,1:T(8,128)(2,1)}), bf16[8,16,768]{2,0,1:T(8,128)(2,1)S(1)}, u32[]{:S(2)}, u32[]{:S(2)}) async-start(bf16[8,16,768]{2,0,1:T(8,128)(2,1)} %bitcast.74), calls=%async_computation | async-start | bytes 393216 | tf_op jit(solution)/shard_map/all_to_all | solution.py:29
  44.8 0.0 reduce-scatter.4.cloned.1.call-start
  45.5 1.3 copy.46
  46.8 0.0 copy-start.1
  46.8 59.9 %all_gather.7 = bf16[2048,64]{0,1:T(8,128)(2,1)S(1)} all-gather(bf16[128,64]{0,1:T(8,128)(2,1)} %param.10), channel_id=1, replica_groups=mesh['dp'=32,'sp'=16] {'sp'}, dimensions={0}, use_global_device_ids=true | all-gather | bytes 278528 | tf_op jit(solution)/shard_map/all_gather | solution.py:52
  106.7 0.0 copy-done
  106.7 1.1 convolution_convert_fusion.2
  107.8 0.0 all-to-all-done
  107.8 0.2 reshape.56
  108.1 0.1 copy.34
  108.3 0.3 convolution_convert_fusion.3
  108.6 5.1 %all-gather.2.cloned.1.call-done = bf16[2048,512]{1,0:T(8,128)(2,1)} async-done(((bf16[128,512]{1,0:T(8,128)(2,1)}), bf16[2048,512]{1,0:T(8,128)(2,1)}) %all-gather.2.cloned.1.call-update) | async-done | bytes 2097168 | tf_op jit(solution)/shard_map/all_gather | solution.py:51
  113.7 2.9 %fusion.14 = f32[512,2048]{1,0:T(8,128)S(1)} fusion(bf16[512,512]{1,0:T(8,128)(2,1)S(1)} %bitcast.61, bf16[2048,512]{1,0:T(8,128)(2,1)} %all-gather.2.cloned.1.call-done), kind=kOutput, calls=%fused_computation.31 | convolution fusion | flops 1073741824 | bytes 6815744 | tf_op jit(solution)/shard_map/dot_general | solution.py:13
  116.6 0.0 copy-done.1
  116.6 1.3 select_reduce_fusion
  117.9 0.0 copy-start.3
  117.9 0.0 copy-start.4
  117.9 1.1 fusion.1
  119.0 0.5 copy-done.3
  119.5 0.1 copy-done.4
  119.6 1.9 multiply_reduce_fusion
  121.5 2.2 multiply_convert_fusion
  123.6 0.5 convolution_convert_fusion
  124.1 1.3 fusion.15
  125.5 2.0 add_convert_fusion
  127.4 1.6 pad_maximum_fusion
  129.0 4.3 %copy.41 = bf16[2048,576]{1,0:T(8,128)(2,1)} copy(bf16[2048,576]{0,1:T(8,128)(2,1)} %pad_maximum_fusion) | data formatting | bytes 4718592
  133.3 0.0 reduce-scatter.4.cloned.1.call-update
  133.4 0.8 fusion.4
  134.1 0.0 copy-start.2
  134.2 2.9 %convolution_convert_fusion.1 = bf16[512,512]{1,0:T(8,128)(2,1)S(1)} fusion(bf16[512,2048]{1,0:T(8,128)(2,1)S(1)} %multiply_convert_fusion, bf16[2048,512]{1,0:T(8,128)(2,1)} %all-gather.2.cloned.1.call-done), kind=kOutput, calls=%fused_computation.12 | convolution fusion | flops 1074003968 | bytes 4718592 | tf_op jit(solution)/shard_map/dot_general | solution.py:65
  137.1 0.0 copy-done.2
  137.1 0.3 fusion.3
  137.4 0.2 copy.39
  137.6 0.2 all_to_all.44
  137.8 19.2 %all_to_all.52 = bf16[16,8,768]{2,1,0:T(8,128)(2,1)S(1)} all-to-all(bf16[16,8,768]{2,1,0:T(8,128)(2,1)S(1)} %all_to_all.44), channel_id=1, replica_groups=mesh['dp'=32,'sp'=16] {'sp'}, dimensions={0} | all-to-all | bytes 393216 | tf_op jit(solution)/shard_map/all_to_all | solution.py:83
  157.0 100.1 %reduce-scatter.4.cloned.1.call-done = bf16[128,576]{1,0:T(8,128)(2,1)} async-done(((bf16[2048,576]{1,0:T(8,128)(2,1)}), bf16[128,576]{1,0:T(8,128)(2,1)}) %reduce-scatter.4.cloned.1.call-update) | async-done | bytes 147472
  257.2 0.8 slice.21
  257.9 0.7 copy.45
  258.6 1.6 slice.20
  260.2 0.7 copy.72
  (6 shorter events, 0.2 us)
Async XLA Ops:
  7.2 99.5 %copy-start = (bf16[512,512]{1,0:T(8,128)(2,1)S(1)}, bf16[512,512]{1,0:T(8,128)(2,1)}, u32[]{:S(2)}) copy-start(bf16[512,512]{1,0:T(8,128)(2,1)} %param.12) | copy-start | bytes 1572868
  7.2 106.5 %all-gather.2.cloned.1.call-start = ((), (), s32[]{:S(2)}) async-start(), calls=%async_computation.4 | async-start | bytes 2228224 | tf_op jit(solution)/shard_map/all_gather | solution.py:51
  41.3 66.5 %all-to-all-start = ((bf16[8,16,768]{2,0,1:T(8,128)(2,1)}), bf16[8,16,768]{2,0,1:T(8,128)(2,1)S(1)}, u32[]{:S(2)}, u32[]{:S(2)}) async-start(bf16[8,16,768]{2,0,1:T(8,128)(2,1)} %bitcast.74), calls=%async_computation | async-start | bytes 393216 | tf_op jit(solution)/shard_map/all_to_all | solution.py:29
  44.8 212.4 %reduce-scatter.4.cloned.1.call-start = ((), (), s32[]{:S(2)}) async-start(), calls=%async_computation.5 | async-start | bytes 2785280
  46.8 69.8 %copy-start.1 = (bf16[512,512]{0,1:T(8,128)(2,1)}, bf16[512,512]{0,1:T(8,128)(2,1)S(1)}, u32[]{:S(2)}) copy-start(bf16[512,512]{0,1:T(8,128)(2,1)S(1)} %copy.46) | copy-start | bytes 1572868
  117.9 1.6 copy-start.3
  117.9 1.7 copy-start.4
  134.1 2.9 %copy-start.2 = (bf16[512,512]{0,1:T(8,128)(2,1)S(1)}, bf16[512,512]{0,1:T(8,128)(2,1)}, u32[]{:S(2)}) copy-start(bf16[512,512]{0,1:T(8,128)(2,1)} %copy-done.1) | copy-start | bytes 1572868
Sparse Core Ops, SparseCore 0:
  11.3 102.3 all-gather.1
  133.5 123.6 reduce-scatter.3
where the time goes:
time: 268 us
  blocking collectives  112 us (42%)
  waiting for transfers between devices  106 us (40%)
  matrix products  15.2 us (6%)
  between operations  14.9 us (6%)
  local copies, waits for them, and re-layouts  10.8 us (4%)
  other arithmetic  4.87 us (2%)
  starting transfers between devices  3.6 us (1%)
    unnamed x3, waiting for transfers between devices  101 us
    all_gather x1, blocking collectives, on_device(): lax.all_gather(rope_key, 'sp', axis=0, tiled=True)  59.9 us
    all_to_all x1, blocking collectives, on_device(): lax.all_to_all(grad_out, 'sp', split_axis=1, concat_axis=0, tiled=True)  33.4 us
    all_to_all x1, blocking collectives, on_device(): lax.all_to_all(d_heads, 'sp', split_axis=0, concat_axis=1, tiled=True)  19.2 us
    unnamed x13, local copies, waits for them, and re-layouts  6.3 us
    dot_general x3, matrix products, contract(): lax.dot_general(left, right, (((1,), (1,)), ((), ())), preferred_element_...  6.06 us
  transfers between devices with their start and end apart: 3, of which 2 were waited for; matrix products, arithmetic and copies ran while one was open for 3% of the time, Pallas kernels for 0%

commit v1 on v0

v1 whole, which is shorter than its diff:
```python
import jax
import jax.numpy as jnp
from jax import lax
from jax.experimental import pallas as pl
from jax.experimental.pallas import tpu as pltpu
from jax.sharding import Mesh, PartitionSpec as P

NOPE = 128
ROPE = 64
VDIM = 128
LATENT = 512
WIDTH = NOPE + ROPE
KEYED = LATENT + ROPE
N_Y, N_Z, N_C = 4, 2, 2
SWAP = [(0, 1), (1, 0)]


def dot(left, right, left_dim, right_dim):
    return lax.dot_general(
        left,
        right,
        (((left_dim,), (right_dim,)), ((), ())),
        preferred_element_type=jnp.float32,
    )


def attention_kernel(
    bound_ref,
    qg_ref,
    wk_ref,
    wv_ref,
    k00_ref,
    k01_ref,
    k10_ref,
    k11_ref,
    d00_ref,
    d01_ref,
    d10_ref,
    d11_ref,
    dq_ref,
    q_cat,
    o_lat,
    rel,
    expo,
    dprob,
):
    scale = WIDTH ** (-0.5)
    count = qg_ref.shape[0]
    heads = wk_ref.shape[1] // NOPE
    stacked = heads * count
    block = k00_ref.shape[0] // N_Y
    keys = (k00_ref, k01_ref, k10_ref, k11_ref)
    d_keys = (d00_ref, d01_ref, d10_ref, d11_ref)

    rel[...] = lax.broadcasted_iota(jnp.int32, rel.shape, 0) - lax.rem(
        lax.broadcasted_iota(jnp.int32, rel.shape, 1), count
    )
    for h in range(heads):
        rows = slice(h * count, (h + 1) * count)
        cols = slice(h * NOPE, (h + 1) * NOPE)
        plain = qg_ref[:, h * WIDTH : h * WIDTH + NOPE]
        grad = qg_ref[:, heads * WIDTH + h * VDIM : heads * WIDTH + (h + 1) * VDIM]
        q_cat[rows, :LATENT] = dot(plain, wk_ref[:, cols], 1, 1).astype(jnp.bfloat16)
        q_cat[rows, LATENT:] = qg_ref[:, h * WIDTH + NOPE : (h + 1) * WIDTH]
        o_lat[rows, :] = dot(grad, wv_ref[:, cols], 1, 1).astype(jnp.bfloat16)

    top = jnp.full((1, stacked), -1e30, jnp.float32)
    total = jnp.zeros((1, stacked), jnp.float32)
    delta = jnp.zeros((1, stacked), jnp.float32)
    tops = []
    for n, key_ref in enumerate(keys):
        base = n * N_Y * block
        scores = dot(key_ref[...], q_cat[...], 1, 1) * scale
        dp = dot(key_ref[:, :LATENT], o_lat[...], 1, 1)
        dprob[base : base + N_Y * block, :] = dp
        visible = [rel[...] <= bound_ref[n * N_Y + j] for j in range(N_Y)]
        parts = [
            jnp.where(visible[j], scores[j * block : (j + 1) * block], -1e30)
            for j in range(N_Y)
        ]
        new_top = top
        for part in parts:
            new_top = jnp.maximum(new_top, jnp.max(part, axis=0, keepdims=True))
        keep = jnp.exp(top - new_top)
        total = total * keep
        delta = delta * keep
        for j, part in enumerate(parts):
            e = jnp.where(visible[j], jnp.exp(part - new_top), 0.0)
            expo[base + j * block : base + (j + 1) * block, :] = e
            total += jnp.sum(e, axis=0, keepdims=True)
            delta += jnp.sum(e * dp[j * block : (j + 1) * block], axis=0, keepdims=True)
        top = new_top
        tops.append(new_top)

    inverse = 1.0 / total
    delta = delta * inverse
    dq_lat = jnp.zeros((stacked, KEYED), jnp.float32)
    for n, (key_ref, d_ref) in enumerate(zip(keys, d_keys)):
        base = n * N_Y * block
        span = slice(base, base + N_Y * block)
        probs = expo[span, :] * (jnp.exp(tops[n] - top) * inverse)
        dscore = (probs * (dprob[span, :] - delta) * scale).astype(jnp.bfloat16)
        probs_low = probs.astype(jnp.bfloat16)
        d_key = dot(dscore, q_cat[...], 1, 0)
        d_ref[:, :LATENT] = (
            d_key[:, :LATENT] + dot(probs_low, o_lat[...], 1, 0)
        ).astype(jnp.bfloat16)
        d_ref[:, LATENT:] = d_key[:, LATENT:].astype(jnp.bfloat16)
        dq_lat += dot(dscore, key_ref[...], 0, 0)
    dq_low = dq_lat.astype(jnp.bfloat16)
    for h in range(heads):
        rows = slice(h * count, (h + 1) * count)
        cols = slice(h * NOPE, (h + 1) * NOPE)
        dq_ref[:, h * WIDTH : h * WIDTH + NOPE] = dot(
            dq_low[rows, :LATENT], wk_ref[:, cols], 1, 0
        ).astype(jnp.bfloat16)
        dq_ref[:, h * WIDTH + NOPE : (h + 1) * WIDTH] = dq_low[rows, LATENT:]


def attention(bounds, qg, w_key, w_value, keys):
    count = qg.shape[0]
    heads = w_key.shape[1] // NOPE
    stacked = heads * count
    chunk = keys[0].shape[0]
    total = len(keys) * chunk
    vmem = pl.BlockSpec(memory_space=pltpu.VMEM)
    return pl.pallas_call(
        attention_kernel,
        out_shape=[jax.ShapeDtypeStruct((chunk, KEYED), jnp.bfloat16) for _ in keys]
        + [jax.ShapeDtypeStruct((count, heads * WIDTH), jnp.bfloat16)],
        in_specs=[pl.BlockSpec(memory_space=pltpu.SMEM)] + [vmem] * (3 + len(keys)),
        out_specs=[vmem] * (len(keys) + 1),
        scratch_shapes=[
            pltpu.VMEM((stacked, KEYED), jnp.bfloat16),
            pltpu.VMEM((stacked, LATENT), jnp.bfloat16),
            pltpu.VMEM((chunk // N_Y, stacked), jnp.int32),
            pltpu.VMEM((total, stacked), jnp.float32),
            pltpu.VMEM((total, stacked), jnp.float32),
        ],
        compiler_params=pltpu.CompilerParams(vmem_limit_bytes=48 * 2**20),
        cost_estimate=pl.CostEstimate(
            flops=2 * total * stacked * (3 * KEYED + 2 * LATENT),
            bytes_accessed=4 * total * KEYED,
            transcendentals=total * stacked,
        ),
    )(bounds, qg, w_key, w_value, *keys)


def shift(block, by):
    return lax.ppermute(block, "y", [(i, (i + by) % N_Y) for i in range(N_Y)])


def gather_y(block):
    return jnp.concatenate([block] + [shift(block, s) for s in range(1, N_Y)], axis=0)


def scatter_y(mine, other):
    block = mine.shape[0] // N_Y
    parts = []
    for s in range(N_Y):
        span = slice(s * block, (s + 1) * block)
        parts.append(
            (mine[span].astype(jnp.float32) + other[span].astype(jnp.float32)).astype(
                jnp.bfloat16
            )
        )
    summed = parts[0].astype(jnp.float32)
    for s in range(1, N_Y):
        summed += shift(parts[s], -s).astype(jnp.float32)
    return summed


def on_device(query, grad_out, latent, rope_key, w_key, w_value, offset):
    rows = query.shape[0]
    n_sp = N_Y * N_Z * N_C
    block = latent.shape[0]
    keyed = jnp.concatenate([latent, rope_key], axis=1)
    far = lax.ppermute(keyed, "z", SWAP)
    qg = jnp.concatenate(
        [query.reshape(rows, n_sp, -1), grad_out.reshape(rows, n_sp, -1)], axis=2
    ).reshape(rows, -1)
    qg = lax.all_to_all(qg, ("y", "z", "c"), split_axis=1, concat_axis=0, tiled=True)
    near_mine = gather_y(keyed)
    near_other = lax.ppermute(near_mine, "c", SWAP)
    far_mine = gather_y(far)
    far_other = lax.ppermute(far_mine, "c", SWAP)
    y, z, c = lax.axis_index("y"), lax.axis_index("z"), lax.axis_index("c")
    starts = []
    for dz, dc in ((1, 1), (1, 0), (0, 1), (0, 0)):
        for s in range(N_Y):
            slot = (lax.rem(y - s + N_Y, N_Y) * N_Z + (z ^ dz)) * N_C + (c ^ dc)
            starts.append(slot * block)
    bounds = offset[0] - jnp.stack(starts).astype(jnp.int32)
    d_far_other, d_far_mine, d_near_other, d_near_mine, dq = attention(
        bounds, qg, w_key, w_value, (far_other, far_mine, near_other, near_mine)
    )
    far_got = lax.ppermute(d_far_other, "c", SWAP)
    near_got = lax.ppermute(d_near_other, "c", SWAP)
    d_query = lax.all_to_all(dq, ("y", "z", "c"), split_axis=0, concat_axis=1, tiled=True)
    far_sum = scatter_y(d_far_mine, far_got).astype(jnp.bfloat16)
    back = lax.ppermute(far_sum, "z", SWAP)
    near_sum = scatter_y(d_near_mine, near_got)
    summed = near_sum + back.astype(jnp.float32)
    d_latent = summed[:, :LATENT].astype(jnp.bfloat16)
    d_rope_key = summed[:, LATENT:].astype(jnp.bfloat16)
    return (d_query, d_latent, d_rope_key)


def solution(mesh):
    parts = mesh.devices.shape[0]
    split = Mesh(
        mesh.devices.reshape(parts, N_Y, N_Z, N_C), ("dp", "y", "z", "c")
    )
    rows = P(("dp", "y", "z", "c"), None)
    columns = P(None, ("y", "z", "c"))
    return jax.shard_map(
        on_device,
        mesh=split,
        in_specs=(rows, rows, rows, rows, columns, columns, P("dp")),
        out_specs=(rows, rows, rows),
        check_vma=False,
    )
```

time: 268 us -> 158 us (0.59)
  the two profiles are of different devices: /device:TPU:4 before, /device:TPU:450 now
where the time goes in v1:
time: 158 us; the launch traced here: 157 us
  starting transfers between devices  83.8 us (53%)
  waiting for transfers between devices  38.7 us (24%)
  local copies, waits for them, and re-layouts  16.7 us (11%)
  Pallas kernels  10.7 us (7%)
  other arithmetic  4.89 us (3%)
  between operations  1.73 us (1%)
    ppermute x12, starting transfers between devices, shift(): return lax.ppermute(block, 'y', [(i, (i + by) % N_Y) for i in range(N_Y)])  40.9 us
    ppermute x1, waiting for transfers between devices, on_device(): back = lax.ppermute(far_sum, 'z', SWAP)  21.7 us
    all_to_all x1, starting transfers between devices, on_device(): lax.all_to_all(qg, ('y', 'z', 'c'), split_axis=1, concat_axis=0, tiled=True)  13.7 us
    all_to_all x1, starting transfers between devices, on_device(): lax.all_to_all(dq, ('y', 'z', 'c'), split_axis=0, concat_axis=1, tiled=True)  13.1 us
    pallas_call x1, Pallas kernels, attention(): pl.pallas_call(attention_kernel, out_shape=[jax.ShapeDtypeStruct((chunk,...  10.7 us
    unnamed x32, local copies, waits for them, and re-layouts  9.49 us
    ppermute x12, waiting for transfers between devices, shift(): return lax.ppermute(block, 'y', [(i, (i + by) % N_Y) for i in range(N_Y)])  8.05 us
    ppermute x1, waiting for transfers between devices, on_device(): far = lax.ppermute(keyed, 'z', SWAP)  7.75 us
  transfers between devices with their start and end apart: 20, of which 5 were waited for; matrix products, arithmetic and copies ran while one was open for 6% of the time, Pallas kernels for 0%

profile of v1, /device:TPU:450, one launch (start us, length us, event | category | flops | bytes accessed | tf_op | source)
XLA Modules:
  0.0 156.5 jit_solution(3120463720087105701)
XLA Ops:
  0.6 0.8 copy.12
  1.5 0.9 pad_maximum_fusion.2
  2.4 4.9 %collective-permute-start.7 = (bf16[128,576]{1,0:T(8,128)(2,1)S(1)}, bf16[128,576]{1,0:T(8,128)(2,1)S(1)}, u32[]{:S(2)}, u32[]{:S(2)}) collective-permute-start(bf16[128,576]{1,0:T(8,128)(2,1)S(1)} %pad_maximum_fusion.2), channel_id=1, source_target_pairs={{0,12},{4,0},{8,4},{12,8},{1,13},{5,1},{9,5},{13,9},{2,14},{6,2},{... | collective-permute-start | bytes 442376 | tf_op jit(solution)/shard_map/ppermute | solution.py:150
  7.3 2.5 %collective-permute-start.6 = (bf16[128,576]{1,0:T(8,128)(2,1)S(1)}, bf16[128,576]{1,0:T(8,128)(2,1)S(1)}, u32[]{:S(2)}, u32[]{:S(2)}) collective-permute-start(bf16[128,576]{1,0:T(8,128)(2,1)S(1)} %pad_maximum_fusion.2), channel_id=1, source_target_pairs={{0,8},{4,12},{8,0},{12,4},{1,9},{5,13},{9,1},{13,5},{2,10},{6,14},... | collective-permute-start | bytes 442376 | tf_op jit(solution)/shard_map/ppermute | solution.py:150
  9.9 2.9 %collective-permute-start.5 = (bf16[128,576]{1,0:T(8,128)(2,1)S(1)}, bf16[128,576]{1,0:T(8,128)(2,1)S(1)}, u32[]{:S(2)}, u32[]{:S(2)}) collective-permute-start(bf16[128,576]{1,0:T(8,128)(2,1)S(1)} %pad_maximum_fusion.2), channel_id=1, source_target_pairs={{0,4},{4,8},{8,12},{12,0},{1,5},{5,9},{9,13},{13,1},{2,6},{6,10},{... | collective-permute-start | bytes 442376 | tf_op jit(solution)/shard_map/ppermute | solution.py:150
  12.8 5.4 %collective-permute-start = (bf16[128,576]{1,0:T(8,128)(2,1)S(1)}, bf16[128,576]{1,0:T(8,128)(2,1)S(1)}, u32[]{:S(2)}, u32[]{:S(2)}) collective-permute-start(bf16[128,576]{1,0:T(8,128)(2,1)S(1)} %pad_maximum_fusion.2), channel_id=1, source_target_pairs={{0,2},{2,0},{1,3},{3,1},{4,6},{6,4},{5,7},{7,5},{8,10},{10,8},{9,1... | collective-permute-start | bytes 442376 | tf_op jit(solution)/shard_map/ppermute | solution.py:178
  18.2 1.8 %pad_maximum_fusion.1 = bf16[8,16,1280]{2,0,1:T(8,128)(2,1)} fusion(bf16[8,16,512]{2,0,1:T(8,128)(2,1)} %bitcast.30, bf16[8,16,768]{2,0,1:T(8,128)(2,1)} %bitcast.29), kind=kLoop, calls=%fused_computation.1 | loop fusion | flops 655360 | bytes 655360 | tf_op jit(solution)/shard_map/concatenate | solution.py:179
  20.0 13.7 %all-to-all-start = ((bf16[8,16,1280]{2,0,1:T(8,128)(2,1)}), bf16[8,16,1280]{2,0,1:T(8,128)(2,1)S(1)}, u32[]{:S(2)}, u32[]{:S(2)}) async-start(bf16[8,16,1280]{2,0,1:T(8,128)(2,1)} %pad_maximum_fusion.1), calls=%async_computation | async-start | bytes 655360 | tf_op jit(solution)/shard_map/all_to_all | solution.py:182
  33.7 7.8 %collective-permute-done = bf16[128,576]{1,0:T(8,128)(2,1)S(1)} collective-permute-done((bf16[128,576]{1,0:T(8,128)(2,1)S(1)}, bf16[128,576]{1,0:T(8,128)(2,1)S(1)}, u32[]{:S(2)}, u32[]{:S(2)}) %collective-permute-start) | collective-permute-done | bytes 147488 | tf_op jit(solution)/shard_map/ppermute | solution.py:178
  41.5 3.7 %collective-permute-start.1 = (bf16[128,576]{1,0:T(8,128)(2,1)S(1)}, bf16[128,576]{1,0:T(8,128)(2,1)S(1)}, u32[]{:S(2)}, u32[]{:S(2)}) collective-permute-start(bf16[128,576]{1,0:T(8,128)(2,1)S(1)} %collective-permute-done), channel_id=1, source_target_pairs={{0,4},{4,8},{8,12},{12,0},{1,5},{5,9},{9,13},{13,1},{2,6},{6,10},{... | collective-permute-start | bytes 442376 | tf_op jit(solution)/shard_map/ppermute | solution.py:150
  45.3 0.2 copy.14
  45.6 1.9 %collective-permute-start.8 = (bf16[512,576]{0,1:T(8,128)(2,1)S(1)}, bf16[512,576]{0,1:T(8,128)(2,1)S(1)}, u32[]{:S(2)}, u32[]{:S(2)}) collective-permute-start(bf16[512,576]{0,1:T(8,128)(2,1)S(1)} %copy.14), channel_id=1, source_target_pairs={{0,1},{1,0},{2,3},{3,2},{4,5},{5,4},{6,7},{7,6},{8,9},{9,8},{10,11... | collective-permute-start | bytes 1769480 | tf_op jit(solution)/shard_map/ppermute | solution.py:184
  47.5 3.3 %collective-permute-start.3 = (bf16[128,576]{1,0:T(8,128)(2,1)S(1)}, bf16[128,576]{1,0:T(8,128)(2,1)S(1)}, u32[]{:S(2)}, u32[]{:S(2)}) collective-permute-start(bf16[128,576]{1,0:T(8,128)(2,1)S(1)} %collective-permute-done), channel_id=1, source_target_pairs={{0,12},{4,0},{8,4},{12,8},{1,13},{5,1},{9,5},{13,9},{2,14},{6,2},{... | collective-permute-start | bytes 442376 | tf_op jit(solution)/shard_map/ppermute | solution.py:150
  50.8 3.2 %collective-permute-start.2 = (bf16[128,576]{1,0:T(8,128)(2,1)S(1)}, bf16[128,576]{1,0:T(8,128)(2,1)S(1)}, u32[]{:S(2)}, u32[]{:S(2)}) collective-permute-start(bf16[128,576]{1,0:T(8,128)(2,1)S(1)} %collective-permute-done), channel_id=1, source_target_pairs={{0,8},{4,12},{8,0},{12,4},{1,9},{5,13},{9,1},{13,5},{2,10},{6,14},... | collective-permute-start | bytes 442376 | tf_op jit(solution)/shard_map/ppermute | solution.py:150
  54.1 6.4 %collective-permute-done.2 = bf16[128,576]{1,0:T(8,128)(2,1)S(1)} collective-permute-done((bf16[128,576]{1,0:T(8,128)(2,1)S(1)}, bf16[128,576]{1,0:T(8,128)(2,1)S(1)}, u32[]{:S(2)}, u32[]{:S(2)}) %collective-permute-start.2) | collective-permute-done | bytes 147488 | tf_op jit(solution)/shard_map/ppermute | solution.py:150
  60.6 1.1 copy.13
  61.7 1.9 %collective-permute-start.4 = (bf16[512,576]{0,1:T(8,128)(2,1)}, bf16[512,576]{0,1:T(8,128)(2,1)}, u32[]{:S(2)}, u32[]{:S(2)}) collective-permute-start(bf16[512,576]{0,1:T(8,128)(2,1)} %copy.13), channel_id=1, source_target_pairs={{0,1},{1,0},{2,3},{3,2},{4,5},{5,4},{6,7},{7,6},{8,9},{9,8},{10,11... | collective-permute-start | bytes 1769480 | tf_op jit(solution)/shard_map/ppermute | solution.py:186
  64.4 0.3 copy.16.k10_ref
  64.7 1.2 collective-permute-done.4
  65.9 1.4 copy.15.k00_ref
  67.3 0.7 copy-done.3
  68.1 1.0 copy-done.4
  69.0 1.0 copy-done.5
  70.1 1.0 copy-done.6
  71.1 10.7 %shard_map.94 = (bf16[512,576]{1,0:T(8,128)(2,1)S(1)}, bf16[512,576]{1,0:T(8,128)(2,1)S(1)}, bf16[512,576]{1,0:T(8,128)(2,1)S(1)}, bf16[512,576]{1,0:T(8,128)(2,1)S(1)}, bf16[128,768]{1,0:T(8,128)(2,1)}) custom-call(s32[16]{0:T(128)S(1)} %broadcast_subtract_fusion.bound_ref, bf16[128,1280]{1,0:T(8,128)(2,1)S(1)} %bitcast.27, bf16[512,512]{1,0:T(8,128)(2,1)S(1)} %copy-done.5, ...), custom_call_target="tpu_custom_call" | custom-call | flops 5771362304 | bytes 4718592 | tf_op jit(solution)/shard_map/pallas_call | solution.py:127
  81.8 0.9 copy-done
  82.7 0.8 copy-done.1
  83.5 2.1 %copy.22 = bf16[512,576]{0,1:T(8,128)(2,1)} copy(bf16[512,576]{1,0:T(8,128)(2,1)} %copy-done) | data formatting | bytes 1179648 | tf_op jit(solution)/shard_map/pallas_call | solution.py:127
  85.6 2.0 %collective-permute-start.13 = (bf16[512,576]{0,1:T(8,128)(2,1)}, bf16[512,576]{0,1:T(8,128)(2,1)S(1)}, u32[]{:S(2)}, u32[]{:S(2)}) collective-permute-start(bf16[512,576]{0,1:T(8,128)(2,1)} %copy.22), channel_id=1, source_target_pairs={{0,1},{1,0},{2,3},{3,2},{4,5},{5,4},{6,7},{7,6},{8,9},{9,8},{10,11... | collective-permute-start | bytes 1769480 | tf_op jit(solution)/shard_map/ppermute | solution.py:197
  87.7 1.1 copy.17
  88.8 2.3 %collective-permute-start.9 = (bf16[512,576]{0,1:T(8,128)(2,1)}, bf16[512,576]{0,1:T(8,128)(2,1)S(1)}, u32[]{:S(2)}, u32[]{:S(2)}) collective-permute-start(bf16[512,576]{0,1:T(8,128)(2,1)} %copy.17), channel_id=1, source_target_pairs={{0,1},{1,0},{2,3},{3,2},{4,5},{5,4},{6,7},{7,6},{8,9},{9,8},{10,11... | collective-permute-start | bytes 1769480 | tf_op jit(solution)/shard_map/ppermute | solution.py:198
  91.1 13.1 %all-to-all-start.1 = ((bf16[16,8,768]{2,1,0:T(8,128)(2,1)}), bf16[16,8,768]{2,1,0:T(8,128)(2,1)S(1)}, u32[]{:S(2)}, u32[]{:S(2)}) async-start(bf16[16,8,768]{2,1,0:T(8,128)(2,1)} %bitcast.21), calls=%async_computation.1 | async-start | bytes 393216 | tf_op jit(solution)/shard_map/all_to_all | solution.py:199
  104.4 0.2 copy.34
  104.9 0.4 copy-done.2
  105.4 0.8 add_convert_fusion.4
  106.1 4.6 %collective-permute-start.14 = (bf16[128,576]{1,0:T(8,128)(2,1)}, bf16[128,576]{1,0:T(8,128)(2,1)S(1)}, u32[]{:S(2)}, u32[]{:S(2)}) collective-permute-start(bf16[128,576]{1,0:T(8,128)(2,1)} %get-tuple-element.22), channel_id=1, source_target_pairs={{0,12},{4,0},{8,4},{12,8},{1,13},{5,1},{9,5},{13,9},{2,14},{6,2},{... | collective-permute-start | bytes 442376 | tf_op jit(solution)/shard_map/ppermute | solution.py:150
  110.7 1.9 %collective-permute-start.16 = (bf16[128,576]{1,0:T(8,128)(2,1)S(1)}, bf16[128,576]{1,0:T(8,128)(2,1)}, u32[]{:S(2)}, u32[]{:S(2)}) collective-permute-start(bf16[128,576]{1,0:T(8,128)(2,1)S(1)} %get-tuple-element.23), channel_id=1, source_target_pairs={{0,4},{4,8},{8,12},{12,0},{1,5},{5,9},{9,13},{13,1},{2,6},{6,10},{... | collective-permute-start | bytes 442376 | tf_op jit(solution)/shard_map/ppermute | solution.py:150
  112.6 4.2 %collective-permute-start.15 = (bf16[128,576]{1,0:T(8,128)(2,1)S(1)}, bf16[128,576]{1,0:T(8,128)(2,1)}, u32[]{:S(2)}, u32[]{:S(2)}) collective-permute-start(bf16[128,576]{1,0:T(8,128)(2,1)S(1)} %get-tuple-element.24), channel_id=1, source_target_pairs={{0,8},{4,12},{8,0},{12,4},{1,9},{5,13},{9,1},{13,5},{2,10},{6,14},... | collective-permute-start | bytes 442376 | tf_op jit(solution)/shard_map/ppermute | solution.py:150
  117.6 3.1 %collective-permute-start.10 = (bf16[128,576]{1,0:T(8,128)(2,1)S(1)}, bf16[128,576]{1,0:T(8,128)(2,1)S(1)}, u32[]{:S(2)}, u32[]{:S(2)}) collective-permute-start(bf16[128,576]{1,0:T(8,128)(2,1)S(1)} %get-tuple-element.19), channel_id=1, source_target_pairs={{0,12},{4,0},{8,4},{12,8},{1,13},{5,1},{9,5},{13,9},{2,14},{6,2},{... | collective-permute-start | bytes 442376 | tf_op jit(solution)/shard_map/ppermute | solution.py:150
  120.7 2.8 %collective-permute-start.12 = (bf16[128,576]{1,0:T(8,128)(2,1)S(1)}, bf16[128,576]{1,0:T(8,128)(2,1)S(1)}, u32[]{:S(2)}, u32[]{:S(2)}) collective-permute-start(bf16[128,576]{1,0:T(8,128)(2,1)S(1)} %get-tuple-element.20), channel_id=1, source_target_pairs={{0,4},{4,8},{8,12},{12,0},{1,5},{5,9},{9,13},{13,1},{2,6},{6,10},{... | collective-permute-start | bytes 442376 | tf_op jit(solution)/shard_map/ppermute | solution.py:150
  123.5 3.7 %collective-permute-start.11 = (bf16[128,576]{1,0:T(8,128)(2,1)S(1)}, bf16[128,576]{1,0:T(8,128)(2,1)S(1)}, u32[]{:S(2)}, u32[]{:S(2)}) collective-permute-start(bf16[128,576]{1,0:T(8,128)(2,1)S(1)} %get-tuple-element.21), channel_id=1, source_target_pairs={{0,8},{4,12},{8,0},{12,4},{1,9},{5,13},{9,1},{13,5},{2,10},{6,14},... | collective-permute-start | bytes 442376 | tf_op jit(solution)/shard_map/ppermute | solution.py:150
  127.2 1.1 add_convert_fusion.1
  128.3 2.5 %collective-permute-start.17 = (bf16[128,576]{1,0:T(8,128)(2,1)S(1)}, bf16[128,576]{1,0:T(8,128)(2,1)S(1)}, u32[]{:S(2)}, u32[]{:S(2)}) collective-permute-start(bf16[128,576]{1,0:T(8,128)(2,1)S(1)} %add_convert_fusion.1), channel_id=1, source_target_pairs={{0,2},{2,0},{1,3},{3,1},{4,6},{6,4},{5,7},{7,5},{8,10},{10,8},{9,1... | collective-permute-start | bytes 442376 | tf_op jit(solution)/shard_map/ppermute | solution.py:201
  131.0 1.6 %collective-permute-done.12 = bf16[128,576]{1,0:T(8,128)(2,1)S(1)} collective-permute-done((bf16[128,576]{1,0:T(8,128)(2,1)S(1)}, bf16[128,576]{1,0:T(8,128)(2,1)S(1)}, u32[]{:S(2)}, u32[]{:S(2)}) %collective-permute-start.12) | collective-permute-done | bytes 147488 | tf_op jit(solution)/shard_map/ppermute | solution.py:150
  132.6 21.7 %collective-permute-done.17 = bf16[128,576]{1,0:T(8,128)(2,1)S(1)} collective-permute-done((bf16[128,576]{1,0:T(8,128)(2,1)S(1)}, bf16[128,576]{1,0:T(8,128)(2,1)S(1)}, u32[]{:S(2)}, u32[]{:S(2)}) %collective-permute-start.17) | collective-permute-done | bytes 147488 | tf_op jit(solution)/shard_map/ppermute | solution.py:201
  154.5 0.7 slice.82
  155.2 0.7 copy.27
  155.8 0.7 copy.41
  (45 shorter events, 1.9 us)
Async XLA Ops:
  2.4 42.8 %collective-permute-start.7 = (bf16[128,576]{1,0:T(8,128)(2,1)S(1)}, bf16[128,576]{1,0:T(8,128)(2,1)S(1)}, u32[]{:S(2)}, u32[]{:S(2)}) collective-permute-start(bf16[128,576]{1,0:T(8,128)(2,1)S(1)} %pad_maximum_fusion.2), channel_id=1, source_target_pairs={{0,12},{4,0},{8,4},{12,8},{1,13},{5,1},{9,5},{13,9},{2,14},{6,2},{... | collective-permute-start | bytes 442376 | tf_op jit(solution)/shard_map/ppermute | solution.py:150
  7.3 37.9 %collective-permute-start.6 = (bf16[128,576]{1,0:T(8,128)(2,1)S(1)}, bf16[128,576]{1,0:T(8,128)(2,1)S(1)}, u32[]{:S(2)}, u32[]{:S(2)}) collective-permute-start(bf16[128,576]{1,0:T(8,128)(2,1)S(1)} %pad_maximum_fusion.2), channel_id=1, source_target_pairs={{0,8},{4,12},{8,0},{12,4},{1,9},{5,13},{9,1},{13,5},{2,10},{6,14},... | collective-permute-start | bytes 442376 | tf_op jit(solution)/shard_map/ppermute | solution.py:150
  9.9 35.4 %collective-permute-start.5 = (bf16[128,576]{1,0:T(8,128)(2,1)S(1)}, bf16[128,576]{1,0:T(8,128)(2,1)S(1)}, u32[]{:S(2)}, u32[]{:S(2)}) collective-permute-start(bf16[128,576]{1,0:T(8,128)(2,1)S(1)} %pad_maximum_fusion.2), channel_id=1, source_target_pairs={{0,4},{4,8},{8,12},{12,0},{1,5},{5,9},{9,13},{13,1},{2,6},{6,10},{... | collective-permute-start | bytes 442376 | tf_op jit(solution)/shard_map/ppermute | solution.py:150
  12.8 28.7 %collective-permute-start = (bf16[128,576]{1,0:T(8,128)(2,1)S(1)}, bf16[128,576]{1,0:T(8,128)(2,1)S(1)}, u32[]{:S(2)}, u32[]{:S(2)}) collective-permute-start(bf16[128,576]{1,0:T(8,128)(2,1)S(1)} %pad_maximum_fusion.2), channel_id=1, source_target_pairs={{0,2},{2,0},{1,3},{3,1},{4,6},{6,4},{5,7},{7,5},{8,10},{10,8},{9,1... | collective-permute-start | bytes 442376 | tf_op jit(solution)/shard_map/ppermute | solution.py:178
  18.2 27.0 %copy-start.8 = (bf16[128,512]{1,0:T(8,128)(2,1)S(1)}, bf16[128,512]{1,0:T(8,128)(2,1)}, u32[]{:S(2)}) copy-start(bf16[128,512]{1,0:T(8,128)(2,1)} %param.9) | copy-start | bytes 393220
  20.0 47.3 %all-to-all-start = ((bf16[8,16,1280]{2,0,1:T(8,128)(2,1)}), bf16[8,16,1280]{2,0,1:T(8,128)(2,1)S(1)}, u32[]{:S(2)}, u32[]{:S(2)}) async-start(bf16[8,16,1280]{2,0,1:T(8,128)(2,1)} %pad_maximum_fusion.1), calls=%async_computation | async-start | bytes 655360 | tf_op jit(solution)/shard_map/all_to_all | solution.py:182
  41.5 12.6 %collective-permute-start.1 = (bf16[128,576]{1,0:T(8,128)(2,1)S(1)}, bf16[128,576]{1,0:T(8,128)(2,1)S(1)}, u32[]{:S(2)}, u32[]{:S(2)}) collective-permute-start(bf16[128,576]{1,0:T(8,128)(2,1)S(1)} %collective-permute-done), channel_id=1, source_target_pairs={{0,4},{4,8},{8,12},{12,0},{1,5},{5,9},{9,13},{13,1},{2,6},{6,10},{... | collective-permute-start | bytes 442376 | tf_op jit(solution)/shard_map/ppermute | solution.py:150
  45.3 5.5 %copy-start.7 = (bf16[512,576]{1,0:T(8,128)(2,1)}, bf16[512,576]{1,0:T(8,128)(2,1)S(1)}, u32[]{:S(2)}) copy-start(bf16[512,576]{1,0:T(8,128)(2,1)S(1)} %pad_maximum_fusion.k11_ref) | copy-start | bytes 1769476
  45.6 18.9 %collective-permute-start.8 = (bf16[512,576]{0,1:T(8,128)(2,1)S(1)}, bf16[512,576]{0,1:T(8,128)(2,1)S(1)}, u32[]{:S(2)}, u32[]{:S(2)}) collective-permute-start(bf16[512,576]{0,1:T(8,128)(2,1)S(1)} %copy.14), channel_id=1, source_target_pairs={{0,1},{1,0},{2,3},{3,2},{4,5},{5,4},{6,7},{7,6},{8,9},{9,8},{10,11... | collective-permute-start | bytes 1769480 | tf_op jit(solution)/shard_map/ppermute | solution.py:184
  47.5 13.1 %collective-permute-start.3 = (bf16[128,576]{1,0:T(8,128)(2,1)S(1)}, bf16[128,576]{1,0:T(8,128)(2,1)S(1)}, u32[]{:S(2)}, u32[]{:S(2)}) collective-permute-start(bf16[128,576]{1,0:T(8,128)(2,1)S(1)} %collective-permute-done), channel_id=1, source_target_pairs={{0,12},{4,0},{8,4},{12,8},{1,13},{5,1},{9,5},{13,9},{2,14},{6,2},{... | collective-permute-start | bytes 442376 | tf_op jit(solution)/shard_map/ppermute | solution.py:150
  50.8 9.7 %collective-permute-start.2 = (bf16[128,576]{1,0:T(8,128)(2,1)S(1)}, bf16[128,576]{1,0:T(8,128)(2,1)S(1)}, u32[]{:S(2)}, u32[]{:S(2)}) collective-permute-start(bf16[128,576]{1,0:T(8,128)(2,1)S(1)} %collective-permute-done), channel_id=1, source_target_pairs={{0,8},{4,12},{8,0},{12,4},{1,9},{5,13},{9,1},{13,5},{2,10},{6,14},... | collective-permute-start | bytes 442376 | tf_op jit(solution)/shard_map/ppermute | solution.py:150
  61.7 4.2 %collective-permute-start.4 = (bf16[512,576]{0,1:T(8,128)(2,1)}, bf16[512,576]{0,1:T(8,128)(2,1)}, u32[]{:S(2)}, u32[]{:S(2)}) collective-permute-start(bf16[512,576]{0,1:T(8,128)(2,1)} %copy.13), channel_id=1, source_target_pairs={{0,1},{1,0},{2,3},{3,2},{4,5},{5,4},{6,7},{7,6},{8,9},{9,8},{10,11... | collective-permute-start | bytes 1769480 | tf_op jit(solution)/shard_map/ppermute | solution.py:186
  67.3 0.7 copy-start.3
  68.1 1.0 copy-start.4
  69.0 1.0 copy-start.5
  70.1 1.0 copy-start.6
  81.8 0.9 copy-start
  82.7 0.8 copy-start.1
  85.6 18.5 %collective-permute-start.13 = (bf16[512,576]{0,1:T(8,128)(2,1)}, bf16[512,576]{0,1:T(8,128)(2,1)S(1)}, u32[]{:S(2)}, u32[]{:S(2)}) collective-permute-start(bf16[512,576]{0,1:T(8,128)(2,1)} %copy.22), channel_id=1, source_target_pairs={{0,1},{1,0},{2,3},{3,2},{4,5},{5,4},{6,7},{7,6},{8,9},{9,8},{10,11... | collective-permute-start | bytes 1769480 | tf_op jit(solution)/shard_map/ppermute | solution.py:197
  88.8 28.1 %collective-permute-start.9 = (bf16[512,576]{0,1:T(8,128)(2,1)}, bf16[512,576]{0,1:T(8,128)(2,1)S(1)}, u32[]{:S(2)}, u32[]{:S(2)}) collective-permute-start(bf16[512,576]{0,1:T(8,128)(2,1)} %copy.17), channel_id=1, source_target_pairs={{0,1},{1,0},{2,3},{3,2},{4,5},{5,4},{6,7},{7,6},{8,9},{9,8},{10,11... | collective-permute-start | bytes 1769480 | tf_op jit(solution)/shard_map/ppermute | solution.py:198
  91.1 39.9 %all-to-all-start.1 = ((bf16[16,8,768]{2,1,0:T(8,128)(2,1)}), bf16[16,8,768]{2,1,0:T(8,128)(2,1)S(1)}, u32[]{:S(2)}, u32[]{:S(2)}) async-start(bf16[16,8,768]{2,1,0:T(8,128)(2,1)} %bitcast.21), calls=%async_computation.1 | async-start | bytes 393216 | tf_op jit(solution)/shard_map/all_to_all | solution.py:199
  104.3 1.1 copy-start.2
  106.1 17.3 %collective-permute-start.14 = (bf16[128,576]{1,0:T(8,128)(2,1)}, bf16[128,576]{1,0:T(8,128)(2,1)S(1)}, u32[]{:S(2)}, u32[]{:S(2)}) collective-permute-start(bf16[128,576]{1,0:T(8,128)(2,1)} %get-tuple-element.22), channel_id=1, source_target_pairs={{0,12},{4,0},{8,4},{12,8},{1,13},{5,1},{9,5},{13,9},{2,14},{6,2},{... | collective-permute-start | bytes 442376 | tf_op jit(solution)/shard_map/ppermute | solution.py:150
  110.7 16.5 %collective-permute-start.16 = (bf16[128,576]{1,0:T(8,128)(2,1)S(1)}, bf16[128,576]{1,0:T(8,128)(2,1)}, u32[]{:S(2)}, u32[]{:S(2)}) collective-permute-start(bf16[128,576]{1,0:T(8,128)(2,1)S(1)} %get-tuple-element.23), channel_id=1, source_target_pairs={{0,4},{4,8},{8,12},{12,0},{1,5},{5,9},{9,13},{13,1},{2,6},{6,10},{... | collective-permute-start | bytes 442376 | tf_op jit(solution)/shard_map/ppermute | solution.py:150
  112.6 14.6 %collective-permute-start.15 = (bf16[128,576]{1,0:T(8,128)(2,1)S(1)}, bf16[128,576]{1,0:T(8,128)(2,1)}, u32[]{:S(2)}, u32[]{:S(2)}) collective-permute-start(bf16[128,576]{1,0:T(8,128)(2,1)S(1)} %get-tuple-element.24), channel_id=1, source_target_pairs={{0,8},{4,12},{8,0},{12,4},{1,9},{5,13},{9,1},{13,5},{2,10},{6,14},... | collective-permute-start | bytes 442376 | tf_op jit(solution)/shard_map/ppermute | solution.py:150
  117.6 13.4 %collective-permute-start.10 = (bf16[128,576]{1,0:T(8,128)(2,1)S(1)}, bf16[128,576]{1,0:T(8,128)(2,1)S(1)}, u32[]{:S(2)}, u32[]{:S(2)}) collective-permute-start(bf16[128,576]{1,0:T(8,128)(2,1)S(1)} %get-tuple-element.19), channel_id=1, source_target_pairs={{0,12},{4,0},{8,4},{12,8},{1,13},{5,1},{9,5},{13,9},{2,14},{6,2},{... | collective-permute-start | bytes 442376 | tf_op jit(solution)/shard_map/ppermute | solution.py:150
  120.7 11.9 %collective-permute-start.12 = (bf16[128,576]{1,0:T(8,128)(2,1)S(1)}, bf16[128,576]{1,0:T(8,128)(2,1)S(1)}, u32[]{:S(2)}, u32[]{:S(2)}) collective-permute-start(bf16[128,576]{1,0:T(8,128)(2,1)S(1)} %get-tuple-element.20), channel_id=1, source_target_pairs={{0,4},{4,8},{8,12},{12,0},{1,5},{5,9},{9,13},{13,1},{2,6},{6,10},{... | collective-permute-start | bytes 442376 | tf_op jit(solution)/shard_map/ppermute | solution.py:150
  123.5 9.2 %collective-permute-start.11 = (bf16[128,576]{1,0:T(8,128)(2,1)S(1)}, bf16[128,576]{1,0:T(8,128)(2,1)S(1)}, u32[]{:S(2)}, u32[]{:S(2)}) collective-permute-start(bf16[128,576]{1,0:T(8,128)(2,1)S(1)} %get-tuple-element.21), channel_id=1, source_target_pairs={{0,8},{4,12},{8,0},{12,4},{1,9},{5,13},{9,1},{13,5},{2,10},{6,14},... | collective-permute-start | bytes 442376 | tf_op jit(solution)/shard_map/ppermute | solution.py:150
  128.3 26.0 %collective-permute-start.17 = (bf16[128,576]{1,0:T(8,128)(2,1)S(1)}, bf16[128,576]{1,0:T(8,128)(2,1)S(1)}, u32[]{:S(2)}, u32[]{:S(2)}) collective-permute-start(bf16[128,576]{1,0:T(8,128)(2,1)S(1)} %add_convert_fusion.1), channel_id=1, source_target_pairs={{0,2},{2,0},{1,3},{3,1},{4,6},{6,4},{5,7},{7,5},{8,10},{10,8},{9,1... | collective-permute-start | bytes 442376 | tf_op jit(solution)/shard_map/ppermute | solution.py:201

commit v2 on v1

v2 whole, which is shorter than its diff:
```python
import jax
import jax.numpy as jnp
from jax import lax
from jax.experimental import pallas as pl
from jax.experimental.pallas import tpu as pltpu
from jax.sharding import Mesh, PartitionSpec as P

NOPE = 128
ROPE = 64
VDIM = 128
LATENT = 512
LANES = 128
WIDTH = NOPE + ROPE
KEYED = LATENT + ROPE
N_Y, N_Z, N_C = 4, 2, 2
SWAP = [(0, 1), (1, 0)]
BF16 = jnp.bfloat16
F32 = jnp.float32


def dot(left, right, left_dim, right_dim):
    return lax.dot_general(
        left,
        right,
        (((left_dim,), (right_dim,)), ((), ())),
        preferred_element_type=F32,
    )


def attention_kernel(
    bound_ref,
    row_ref,
    slot_ref,
    qg_hbm,
    wk_hbm,
    wv_hbm,
    far_other_hbm,
    far_mine_hbm,
    near_other_hbm,
    near_mine_hbm,
    d_far_other_hbm,
    d_far_mine_hbm,
    d_near_other_hbm,
    d_near_mine_hbm,
    qg_ref,
    wk_ref,
    wv_ref,
    packed,
    keyed,
    d_near,
    d_far,
    dq_ref,
    q_cat,
    o_lat,
    rel,
    expo,
    dprob,
    in_sem,
    out_sem,
):
    scale = WIDTH ** (-0.5)
    count = qg_ref.shape[0]
    heads = wk_ref.shape[1] // NOPE
    stacked = heads * count
    block = rel.shape[0]
    chunk = N_Y * block
    n_chunks = N_Z * N_C
    folds = LATENT // LANES
    tall = ROPE // folds
    slab = folds * block + ROPE
    keys_hbm = (far_other_hbm, far_mine_hbm, near_other_hbm, near_mine_hbm)

    loads = [
        pltpu.make_async_copy(qg_hbm, qg_ref, in_sem.at[0]),
        pltpu.make_async_copy(wk_hbm, wk_ref, in_sem.at[1]),
        pltpu.make_async_copy(wv_hbm, wv_ref, in_sem.at[2]),
    ] + [
        pltpu.make_async_copy(ref, packed.at[n], in_sem.at[3 + n])
        for n, ref in enumerate(keys_hbm)
    ]
    for load in loads:
        load.start()

    rel[...] = lax.broadcasted_iota(jnp.int32, rel.shape, 0) - lax.rem(
        lax.broadcasted_iota(jnp.int32, rel.shape, 1), count
    )
    for load in loads[:3]:
        load.wait()
    for h in range(heads):
        rows = slice(h * count, (h + 1) * count)
        cols = slice(h * NOPE, (h + 1) * NOPE)
        plain = qg_ref[:, h * WIDTH : h * WIDTH + NOPE]
        grad = qg_ref[:, heads * WIDTH + h * VDIM : heads * WIDTH + (h + 1) * VDIM]
        q_cat[rows, :LATENT] = dot(plain, wk_ref[:, cols], 1, 1).astype(BF16)
        q_cat[rows, LATENT:] = qg_ref[:, h * WIDTH + NOPE : (h + 1) * WIDTH]
        o_lat[rows, :] = dot(grad, wv_ref[:, cols], 1, 1).astype(BF16)

    top = jnp.full((1, stacked), -1e30, F32)
    total = jnp.zeros((1, stacked), F32)
    delta = jnp.zeros((1, stacked), F32)
    tops = []
    for n in range(n_chunks):
        loads[3 + n].wait()
        base = n * chunk
        for j in range(N_Y):
            span = slice(base + j * block, base + (j + 1) * block)
            keyed[span, :LATENT] = packed[n, j, :block, :]
            rot = jnp.concatenate(
                [packed[n, j, block:, a * LANES : (a + 1) * LANES] for a in range(folds)],
                axis=0,
            )
            keyed[span, LATENT:] = jnp.transpose(rot)
        span = slice(base, base + chunk)
        scores = dot(keyed[span, :], q_cat[...], 1, 1) * scale
        dp = dot(keyed[span, :LATENT], o_lat[...], 1, 1)
        dprob[span, :] = dp
        visible = [rel[...] <= bound_ref[n * N_Y + j] for j in range(N_Y)]
        parts = [
            jnp.where(visible[j], scores[j * block : (j + 1) * block], -1e30)
            for j in range(N_Y)
        ]
        new_top = top
        for part in parts:
            new_top = jnp.maximum(new_top, jnp.max(part, axis=0, keepdims=True))
        keep = jnp.exp(top - new_top)
        total = total * keep
        delta = delta * keep
        for j, part in enumerate(parts):
            e = jnp.where(visible[j], jnp.exp(part - new_top), 0.0)
            expo[base + j * block : base + (j + 1) * block, :] = e
            total += jnp.sum(e, axis=0, keepdims=True)
            delta += jnp.sum(e * dp[j * block : (j + 1) * block], axis=0, keepdims=True)
        top = new_top
        tops.append(new_top)

    inverse = 1.0 / total
    delta = delta * inverse
    dq_lat = jnp.zeros((stacked, KEYED), F32)
    stores = []
    for n in (2, 3, 0, 1):
        span = slice(n * chunk, (n + 1) * chunk)
        probs = expo[span, :] * (jnp.exp(tops[n] - top) * inverse)
        dscore = (probs * (dprob[span, :] - delta) * scale).astype(BF16)
        probs_low = probs.astype(BF16)
        d_key = dot(dscore, q_cat[...], 1, 0)
        d_lat = (d_key[:, :LATENT] + dot(probs_low, o_lat[...], 1, 0)).astype(BF16)
        d_rot = d_key[:, LATENT:].astype(BF16)
        for j in range(N_Y):
            rows = slice(j * block, (j + 1) * block)
            place = d_far.at[n, slot_ref[j]] if n < 2 else d_near.at[n - 2, slot_ref[j]]
            for a in range(folds):
                place[a * block : (a + 1) * block, :] = d_lat[
                    rows, a * LANES : (a + 1) * LANES
                ]
            place[folds * block : slab, :] = jnp.transpose(d_rot[rows])
        if n >= 2:
            store = pltpu.make_async_copy(
                d_near.at[n - 2],
                (d_near_other_hbm, d_near_mine_hbm)[n - 2],
                out_sem.at[n],
            )
            store.start()
            stores.append(store)
        dq_lat += dot(dscore, keyed[span, :], 0, 0)
    dq_low = dq_lat.astype(BF16)
    for h in range(heads):
        rows = slice(h * count, (h + 1) * count)
        cols = slice(h * NOPE, (h + 1) * NOPE)
        dq_ref[:, h * WIDTH : h * WIDTH + NOPE] = dot(
            dq_low[rows, :LATENT], wk_ref[:, cols], 1, 0
        )
        dq_ref[:, h * WIDTH + NOPE : (h + 1) * WIDTH] = dq_lat[rows, LATENT:]
    few = count // (N_Y * N_Z * N_C)
    for n in range(N_C):
        for j in range(N_Y):
            pieces = []
            for dz in range(N_Z):
                start = pl.multiple_of(row_ref[(n * N_Y + j) * N_Z + dz], few)
                for a in range(heads * WIDTH // LANES):
                    pieces.append(dq_ref[pl.ds(start, few), a * LANES : (a + 1) * LANES])
            d_far[n, j, slab:, :] = jnp.concatenate(pieces, axis=0).astype(BF16)
        store = pltpu.make_async_copy(
            d_far.at[n], (d_far_other_hbm, d_far_mine_hbm)[n], out_sem.at[n]
        )
        store.start()
        stores.append(store)
    for store in stores:
        store.wait()


def attention(bounds, starts, slots, qg, w_key, w_value, far_other, far_mine, near_other, near_mine):
    count = qg.shape[0]
    heads = w_key.shape[1] // NOPE
    stacked = heads * count
    tall = near_mine.shape[1]
    block = tall * LATENT // KEYED
    n_chunks = N_Z * N_C
    total = n_chunks * N_Y * block
    slab = block * KEYED // LANES
    extra = N_Z * (count // (N_Y * N_Z * N_C)) * heads * WIDTH // LANES
    hbm = pl.BlockSpec(memory_space=pl.ANY)
    smem = pl.BlockSpec(memory_space=pltpu.SMEM)
    return pl.pallas_call(
        attention_kernel,
        out_shape=[
            jax.ShapeDtypeStruct((N_Y, slab + extra, LANES), BF16),
            jax.ShapeDtypeStruct((N_Y, slab + extra, LANES), BF16),
            jax.ShapeDtypeStruct((N_Y, slab, LANES), BF16),
            jax.ShapeDtypeStruct((N_Y, slab, LANES), BF16),
        ],
        in_specs=[smem] * 3 + [hbm] * 7,
        out_specs=[hbm] * 4,
        scratch_shapes=[
            pltpu.VMEM(qg.shape, BF16),
            pltpu.VMEM(w_key.shape, BF16),
            pltpu.VMEM(w_value.shape, BF16),
            pltpu.VMEM((n_chunks, N_Y, tall, LATENT), BF16),
            pltpu.VMEM((total, KEYED), BF16),
            pltpu.VMEM((N_C, N_Y, slab, LANES), BF16),
            pltpu.VMEM((N_C, N_Y, slab + extra, LANES), BF16),
            pltpu.VMEM((count, heads * WIDTH), F32),
            pltpu.VMEM((stacked, KEYED), BF16),
            pltpu.VMEM((stacked, LATENT), BF16),
            pltpu.VMEM((block, stacked), jnp.int32),
            pltpu.VMEM((total, stacked), F32),
            pltpu.VMEM((total, stacked), F32),
            pltpu.SemaphoreType.DMA((3 + n_chunks,)),
            pltpu.SemaphoreType.DMA((n_chunks,)),
        ],
        compiler_params=pltpu.CompilerParams(vmem_limit_bytes=56 * 2**20),
        cost_estimate=pl.CostEstimate(
            flops=2 * total * stacked * (3 * KEYED + 2 * LATENT),
            bytes_accessed=4 * total * KEYED,
            transcendentals=total * stacked,
        ),
    )(bounds, starts, slots, qg, w_key, w_value, far_other, far_mine, near_other, near_mine)


def shift(block, by):
    return lax.ppermute(block, "y", [(i, (i + by) % N_Y) for i in range(N_Y)])


def on_device(query, grad_out, latent, rope_key, w_key, w_value, offset):
    few = query.shape[0]
    n_sp = N_Y * N_Z * N_C
    block = latent.shape[0]
    folds = LATENT // LANES
    y, z, c = lax.axis_index("y"), lax.axis_index("z"), lax.axis_index("c")
    turned = rope_key.T.reshape(folds, ROPE // folds, block)
    pack = jnp.concatenate(
        [latent, jnp.transpose(turned, (1, 0, 2)).reshape(-1, LATENT)], axis=0
    )
    far = lax.ppermute(pack, "z", SWAP)
    qg = jnp.concatenate(
        [query.reshape(few, n_sp, -1), grad_out.reshape(few, n_sp, -1)], axis=2
    ).reshape(few, -1)
    qg, pack = lax.optimization_barrier((qg, pack))
    near_mine = [pack] + [shift(pack, s) for s in range(1, N_Y)]
    qg, near_mine[1] = lax.optimization_barrier((qg, near_mine[1]))
    near_mine = jnp.stack(near_mine)
    qg = lax.all_to_all(qg, ("y", "z", "c"), split_axis=1, concat_axis=0, tiled=True)
    near_other = lax.ppermute(near_mine, "c", SWAP)
    far_mine = jnp.stack([far] + [shift(far, s) for s in range(1, N_Y)])
    far_other = lax.ppermute(far_mine, "c", SWAP)

    steps = jnp.arange(N_Y, dtype=jnp.int32)

    def owner(y_of, z_of, c_of):
        return ((y_of * N_Z + z_of) * N_C + c_of).astype(jnp.int32)

    shifted = lax.rem(y - steps + N_Y, N_Y)
    owners = [owner(shifted, z ^ dz, c ^ dc) for dz in (1, 0) for dc in (1, 0)]
    bounds = offset[0] - jnp.concatenate(owners) * block
    starts = jnp.stack(
        [
            owner(steps[:, None], z ^ jnp.array([[1, 0]]), c ^ dc).reshape(-1)
            for dc in (1, 0)
        ]
    ).reshape(-1)
    d_other, d_mine, d_near_other, d_near_mine = attention(
        bounds,
        starts * few,
        shifted.astype(jnp.int32),
        qg,
        w_key,
        w_value,
        far_other,
        far_mine,
        near_other,
        near_mine,
    )
    slab = d_near_mine.shape[1]
    got = lax.ppermute(d_other, "c", SWAP)
    summed = d_mine[:, :slab].astype(F32) + got[:, :slab].astype(F32)
    sent = jnp.concatenate([summed.astype(BF16), d_mine[:, slab:], got[:, slab:]], axis=1)
    sent, d_near_other = lax.optimization_barrier((sent, d_near_other))
    near_got = lax.ppermute(d_near_other, "c", SWAP)
    near_half = (d_near_mine.astype(F32) + near_got.astype(F32)).astype(BF16)
    slots = lax.all_to_all(sent, "y", split_axis=0, concat_axis=0, tiled=True)
    far_sum = jnp.sum(slots[:, :slab].astype(F32), axis=0).astype(BF16)
    piece = (d_mine.shape[1] - slab) // N_Z
    parts = slots[:, slab:].reshape(N_Y, N_C, N_Z, piece, LANES)
    leaving = jnp.concatenate([far_sum, parts[:, :, 0].reshape(-1, LANES)], axis=0)
    back = lax.ppermute(leaving, "z", SWAP)
    _, near_half = lax.optimization_barrier((leaving, near_half))
    near_sum = lax.all_to_all(near_half, "y", split_axis=0, concat_axis=0, tiled=True)
    near_sum = jnp.sum(near_sum.astype(F32), axis=0)
    summed = (near_sum + back[:slab].astype(F32)).astype(BF16)
    d_latent = jnp.transpose(
        summed[: folds * block].reshape(folds, block, LANES), (1, 0, 2)
    ).reshape(block, LATENT)
    d_rope_key = summed[folds * block :].T
    both = jnp.stack(
        [parts[:, :, 1], back[slab:].reshape(N_Y, N_C, piece, LANES)]
    ).reshape(N_Z, N_Y, N_C, -1, few, LANES)
    both = jnp.where(z == 1, both[::-1], both)
    both = jnp.where(c == 1, both[:, :, ::-1], both)
    d_query = jnp.transpose(both, (4, 1, 0, 2, 3, 5)).reshape(few, -1)
    return (d_query, d_latent, d_rope_key)


def solution(mesh):
    parts = mesh.devices.shape[0]
    split = Mesh(mesh.devices.reshape(parts, N_Y, N_Z, N_C), ("dp", "y", "z", "c"))
    rows = P(("dp", "y", "z", "c"), None)
    columns = P(None, ("y", "z", "c"))
    return jax.shard_map(
        on_device,
        mesh=split,
        in_specs=(rows, rows, rows, rows, columns, columns, P("dp")),
        out_specs=(rows, rows, rows),
        check_vma=False,
    )
```

time: 158 us -> 133 us (0.84)
  the two profiles are of different devices: /device:TPU:450 before, /device:TPU:32 now
where the time goes in v2:
time: 133 us; the launch traced here: 132 us
  starting transfers between devices  63.4 us (48%)
  waiting for transfers between devices  41.7 us (31%)
  Pallas kernels  12.7 us (10%)
  other arithmetic  6.59 us (5%)
  local copies, waits for them, and re-layouts  6.18 us (5%)
  between operations  1.66 us (1%)
    ppermute x6, starting transfers between devices, shift(): return lax.ppermute(block, 'y', [(i, (i + by) % N_Y) for i in range(N_Y)])  21 us
    ppermute x1, waiting for transfers between devices, on_device(): back = lax.ppermute(leaving, 'z', SWAP)  19 us
    ppermute x1, starting transfers between devices, on_device(): far = lax.ppermute(pack, 'z', SWAP)  14.8 us
    pallas_call x1, Pallas kernels, attention(): pl.pallas_call(attention_kernel, out_shape=[jax.ShapeDtypeStruct((N_Y, sl...  12.7 us
    all_to_all x1, waiting for transfers between devices, on_device(): slots = lax.all_to_all(sent, 'y', split_axis=0, concat_axis=0, tiled=True)  10.8 us
    ppermute x1, starting transfers between devices, on_device(): back = lax.ppermute(leaving, 'z', SWAP)  9.11 us
    all_to_all x1, waiting for transfers between devices, on_device(): lax.all_to_all(qg, ('y', 'z', 'c'), split_axis=1, concat_axis=0, tiled=True)  4.54 us
    ppermute x6, waiting for transfers between devices, shift(): return lax.ppermute(block, 'y', [(i, (i + by) % N_Y) for i in range(N_Y)])  4.07 us
  transfers between devices with their start and end apart: 15, of which 7 were waited for; matrix products, arithmetic and copies ran while one was open for 4% of the time, Pallas kernels for 0%

profile of v2, /device:TPU:32, one launch (start us, length us, event | category | flops | bytes accessed | tf_op | source)
XLA Modules:
  0.0 132.1 jit_solution(8408850112172598701)
XLA Ops:
  0.6 0.7 copy.15
  1.4 0.9 constant_dynamic-update-slice_fusion
  2.3 1.7 %pad_maximum_fusion.3 = bf16[8,16,1280]{2,0,1:T(8,128)(2,1)} fusion(bf16[8,16,512]{2,0,1:T(8,128)(2,1)} %bitcast.58, bf16[8,16,768]{2,0,1:T(8,128)(2,1)} %bitcast.50), kind=kLoop, calls=%fused_computation.7 | loop fusion | flops 655360 | bytes 655360 | tf_op jit(solution)/shard_map/concatenate | solution.py:254
  4.0 3.5 %collective-permute-start = (bf16[144,512]{1,0:T(8,128)(2,1)S(1)}, bf16[144,512]{1,0:T(8,128)(2,1)S(1)}, u32[]{:S(2)}, u32[]{:S(2)}) collective-permute-start(bf16[144,512]{1,0:T(8,128)(2,1)S(1)} %bitcast_dynamic-update-slice_fusion), channel_id=1, source_target_pairs={{0,4},{4,8},{8,12},{12,0},{1,5},{5,9},{9,13},{13,1},{2,6},{6,10},{... | collective-permute-start | bytes 442376 | tf_op jit(solution)/shard_map/ppermute | solution.py:240
  7.5 14.8 %collective-permute-start.1 = (bf16[144,512]{1,0:T(8,128)(2,1)S(1)}, bf16[144,512]{1,0:T(8,128)(2,1)S(1)}, u32[]{:S(2)}, u32[]{:S(2)}) collective-permute-start(bf16[144,512]{1,0:T(8,128)(2,1)S(1)} %bitcast_dynamic-update-slice_fusion), channel_id=1, source_target_pairs={{0,2},{2,0},{1,3},{3,1},{4,6},{6,4},{5,7},{7,5},{8,10},{10,8},{9,1... | collective-permute-start | bytes 442376 | tf_op jit(solution)/shard_map/ppermute | solution.py:253
  22.3 3.6 %collective-permute-start.7 = (bf16[144,512]{1,0:T(8,128)(2,1)S(1)}, bf16[144,512]{1,0:T(8,128)(2,1)S(1)}, u32[]{:S(2)}, u32[]{:S(2)}) collective-permute-start(bf16[144,512]{1,0:T(8,128)(2,1)S(1)} %bitcast_dynamic-update-slice_fusion), channel_id=1, source_target_pairs={{0,12},{4,0},{8,4},{12,8},{1,13},{5,1},{9,5},{13,9},{2,14},{6,2},{... | collective-permute-start | bytes 442376 | tf_op jit(solution)/shard_map/ppermute | solution.py:240
  25.9 3.9 %collective-permute-start.6 = (bf16[144,512]{1,0:T(8,128)(2,1)S(1)}, bf16[144,512]{1,0:T(8,128)(2,1)S(1)}, u32[]{:S(2)}, u32[]{:S(2)}) collective-permute-start(bf16[144,512]{1,0:T(8,128)(2,1)S(1)} %bitcast_dynamic-update-slice_fusion), channel_id=1, source_target_pairs={{0,8},{4,12},{8,0},{12,4},{1,9},{5,13},{9,1},{13,5},{2,10},{6,14},... | collective-permute-start | bytes 442376 | tf_op jit(solution)/shard_map/ppermute | solution.py:240
  29.8 0.0 collective-permute-done
  29.8 3.6 %all-to-all-start = ((bf16[8,16,1280]{2,0,1:T(8,128)(2,1)}), bf16[8,16,1280]{2,0,1:T(8,128)(2,1)S(1)}, u32[]{:S(2)}, u32[]{:S(2)}) async-start(bf16[8,16,1280]{2,0,1:T(8,128)(2,1)} %bitcast.8), calls=%async_computation | async-start | bytes 655360 | tf_op jit(solution)/shard_map/all_to_all | solution.py:261
  33.4 1.8 %collective-permute-done.1 = bf16[144,512]{1,0:T(8,128)(2,1)S(1)} collective-permute-done((bf16[144,512]{1,0:T(8,128)(2,1)S(1)}, bf16[144,512]{1,0:T(8,128)(2,1)S(1)}, u32[]{:S(2)}, u32[]{:S(2)}) %collective-permute-start.1) | collective-permute-done | bytes 147488 | tf_op jit(solution)/shard_map/ppermute | solution.py:253
  35.3 3.6 %collective-permute-start.4 = (bf16[144,512]{1,0:T(8,128)(2,1)S(1)}, bf16[144,512]{1,0:T(8,128)(2,1)S(1)}, u32[]{:S(2)}, u32[]{:S(2)}) collective-permute-start(bf16[144,512]{1,0:T(8,128)(2,1)S(1)} %collective-permute-done.1), channel_id=1, source_target_pairs={{0,12},{4,0},{8,4},{12,8},{1,13},{5,1},{9,5},{13,9},{2,14},{6,2},{... | collective-permute-start | bytes 442376 | tf_op jit(solution)/shard_map/ppermute | solution.py:240
  38.9 3.8 %collective-permute-start.3 = (bf16[144,512]{1,0:T(8,128)(2,1)S(1)}, bf16[144,512]{1,0:T(8,128)(2,1)S(1)}, u32[]{:S(2)}, u32[]{:S(2)}) collective-permute-start(bf16[144,512]{1,0:T(8,128)(2,1)S(1)} %collective-permute-done.1), channel_id=1, source_target_pairs={{0,8},{4,12},{8,0},{12,4},{1,9},{5,13},{9,1},{13,5},{2,10},{6,14},... | collective-permute-start | bytes 442376 | tf_op jit(solution)/shard_map/ppermute | solution.py:240
  42.7 2.6 %collective-permute-start.2 = (bf16[144,512]{1,0:T(8,128)(2,1)S(1)}, bf16[144,512]{1,0:T(8,128)(2,1)S(1)}, u32[]{:S(2)}, u32[]{:S(2)}) collective-permute-start(bf16[144,512]{1,0:T(8,128)(2,1)S(1)} %collective-permute-done.1), channel_id=1, source_target_pairs={{0,4},{4,8},{8,12},{12,0},{1,5},{5,9},{9,13},{13,1},{2,6},{6,10},{... | collective-permute-start | bytes 442376 | tf_op jit(solution)/shard_map/ppermute | solution.py:240
  45.4 0.0 collective-permute-done.6
  45.4 0.1 pad_maximum_fusion.2.near_mine_hbm
  45.5 1.9 %collective-permute-start.8 = (bf16[4,144,512]{2,1,0:T(8,128)(2,1)S(1)}, bf16[4,144,512]{2,1,0:T(8,128)(2,1)S(1)}, u32[]{:S(2)}, u32[]{:S(2)}) collective-permute-start(bf16[4,144,512]{2,1,0:T(8,128)(2,1)S(1)} %pad_maximum_fusion.2.near_mine_hbm), channel_id=1, source_target_pairs={{0,1},{1,0},{2,3},{3,2},{4,5},{5,4},{6,7},{7,6},{8,9},{9,8},{10,11... | collective-permute-start | bytes 1769480 | tf_op jit(solution)/shard_map/ppermute | solution.py:262
  47.4 1.9 %collective-permute-done.3 = bf16[144,512]{1,0:T(8,128)(2,1)S(1)} collective-permute-done((bf16[144,512]{1,0:T(8,128)(2,1)S(1)}, bf16[144,512]{1,0:T(8,128)(2,1)S(1)}, u32[]{:S(2)}, u32[]{:S(2)}) %collective-permute-start.3) | collective-permute-done | bytes 147488 | tf_op jit(solution)/shard_map/ppermute | solution.py:240
  49.3 2.1 %collective-permute-done.2 = bf16[144,512]{1,0:T(8,128)(2,1)S(1)} collective-permute-done((bf16[144,512]{1,0:T(8,128)(2,1)S(1)}, bf16[144,512]{1,0:T(8,128)(2,1)S(1)}, u32[]{:S(2)}, u32[]{:S(2)}) %collective-permute-start.2) | collective-permute-done | bytes 147488 | tf_op jit(solution)/shard_map/ppermute | solution.py:240
  51.5 0.1 pad_maximum_fusion.1.far_mine_hbm
  51.6 1.9 %collective-permute-start.5 = (bf16[4,144,512]{2,1,0:T(8,128)(2,1)S(1)}, bf16[4,144,512]{2,1,0:T(8,128)(2,1)S(1)}, u32[]{:S(2)}, u32[]{:S(2)}) collective-permute-start(bf16[4,144,512]{2,1,0:T(8,128)(2,1)S(1)} %pad_maximum_fusion.1.far_mine_hbm), channel_id=1, source_target_pairs={{0,1},{1,0},{2,3},{3,2},{4,5},{5,4},{6,7},{7,6},{8,9},{9,8},{10,11... | collective-permute-start | bytes 1769480 | tf_op jit(solution)/shard_map/ppermute | solution.py:264
  53.5 0.1 fusion.2
  54.2 0.1 add.143
  54.3 0.1 add.149
  54.4 0.7 mul.63.row_ref
  55.1 0.5 compare_select_fusion
  55.6 0.6 fusion.4.bound_ref
  56.2 0.0 collective-permute-done.8.near_other_hbm
  56.2 4.5 %all-to-all-done = bf16[8,16,1280]{2,0,1:T(8,128)(2,1)S(1)} async-done(((bf16[8,16,1280]{2,0,1:T(8,128)(2,1)}), bf16[8,16,1280]{2,0,1:T(8,128)(2,1)S(1)}, u32[]{:S(2)}, u32[]{:S(2)}) %all-to-all-start) | async-done | bytes 327712 | tf_op jit(solution)/shard_map/all_to_all | solution.py:261
  60.8 0.7 copy-done.3
  61.5 12.7 %shard_map.112 = (bf16[4,672,128]{2,1,0:T(8,128)(2,1)}, bf16[4,672,128]{2,1,0:T(8,128)(2,1)}, bf16[4,576,128]{2,1,0:T(8,128)(2,1)}, bf16[4,576,128]{2,1,0:T(8,128)(2,1)}) custom-call(s32[16]{0:T(128)} %fusion.4.bound_ref, s32[16]{0:T(128)} %mul.63.row_ref, s32[4]{0:T(128)} %get-tuple-element.31.slot_ref, bf16[128,1280]{1,0:T(8,128)(2,1)} %bitcast.48, ...), custom_call_target="tpu_custom_call" | custom-call | flops 5771362304 | bytes 4718592 | tf_op jit(solution)/shard_map/pallas_call | solution.py:203
  74.2 1.9 %collective-permute-start.9 = (bf16[4,672,128]{2,1,0:T(8,128)(2,1)}, bf16[4,672,128]{2,1,0:T(8,128)(2,1)S(1)}, u32[]{:S(2)}, u32[]{:S(2)}) collective-permute-start(bf16[4,672,128]{2,1,0:T(8,128)(2,1)} %get-tuple-element.19), channel_id=1, source_target_pairs={{0,1},{1,0},{2,3},{3,2},{4,5},{5,4},{6,7},{7,6},{8,9},{9,8},{10,11... | collective-permute-start | bytes 2064392 | tf_op jit(solution)/shard_map/ppermute | solution.py:293
  76.1 0.9 slice.38
  77.0 1.4 %collective-permute-done.9 = bf16[4,672,128]{2,1,0:T(8,128)(2,1)S(1)} collective-permute-done((bf16[4,672,128]{2,1,0:T(8,128)(2,1)}, bf16[4,672,128]{2,1,0:T(8,128)(2,1)S(1)}, u32[]{:S(2)}, u32[]{:S(2)}) %collective-permute-start.9) | collective-permute-done | bytes 688160 | tf_op jit(solution)/shard_map/ppermute | solution.py:293
  78.4 1.2 add_convert_fusion.1
  79.7 0.9 pad_maximum_fusion
  80.6 3.6 %all-to-all-start.1 = ((bf16[4,768,128]{2,1,0:T(8,128)(2,1)}), bf16[4,768,128]{2,1,0:T(8,128)(2,1)S(1)}, u32[]{:S(2)}, u32[]{:S(2)}) async-start(bf16[4,768,128]{2,1,0:T(8,128)(2,1)} %pad_maximum_fusion), calls=%async_computation.1 | async-start | bytes 1572864 | tf_op jit(solution)/shard_map/all_to_all | solution.py:299
  84.2 2.0 %collective-permute-start.11 = (bf16[4,576,128]{2,1,0:T(8,128)(2,1)S(1)}, bf16[4,576,128]{2,1,0:T(8,128)(2,1)S(1)}, u32[]{:S(2)}, u32[]{:S(2)}) collective-permute-start(bf16[4,576,128]{2,1,0:T(8,128)(2,1)S(1)} %copy-done.6), channel_id=1, source_target_pairs={{0,1},{1,0},{2,3},{3,2},{4,5},{5,4},{6,7},{7,6},{8,9},{9,8},{10,11... | collective-permute-start | bytes 1769480 | tf_op jit(solution)/shard_map/ppermute | solution.py:297
  86.3 10.8 %all-to-all-done.1 = bf16[4,768,128]{2,1,0:T(8,128)(2,1)S(1)} async-done(((bf16[4,768,128]{2,1,0:T(8,128)(2,1)}), bf16[4,768,128]{2,1,0:T(8,128)(2,1)S(1)}, u32[]{:S(2)}, u32[]{:S(2)}) %all-to-all-start.1) | async-done | bytes 786464 | tf_op jit(solution)/shard_map/all_to_all | solution.py:299
  97.1 0.1 slice_reduce_fusion
  97.2 9.1 %collective-permute-start.10 = (bf16[960,128]{1,0:T(8,128)(2,1)S(1)}, bf16[960,128]{1,0:T(8,128)(2,1)S(1)}, u32[]{:S(2)}, u32[]{:S(2)}) collective-permute-start(bf16[960,128]{1,0:T(8,128)(2,1)S(1)} %pad_maximum_fusion.4), channel_id=1, source_target_pairs={{0,2},{2,0},{1,3},{3,1},{4,6},{6,4},{5,7},{7,5},{8,10},{10,8},{9,1... | collective-permute-start | bytes 737288 | tf_op jit(solution)/shard_map/ppermute | solution.py:304
  106.4 1.0 add_convert_fusion
  107.4 3.5 %all-to-all-start.2 = ((bf16[4,576,128]{2,1,0:T(8,128)(2,1)}), bf16[4,576,128]{2,1,0:T(8,128)(2,1)S(1)}, u32[]{:S(2)}, u32[]{:S(2)}) async-start(bf16[4,576,128]{2,1,0:T(8,128)(2,1)} %add_convert_fusion), calls=%async_computation.2 | async-start | bytes 1179648 | tf_op jit(solution)/shard_map/all_to_all | solution.py:306
  110.8 19.0 %collective-permute-done.10 = bf16[960,128]{1,0:T(8,128)(2,1)S(1)} collective-permute-done((bf16[960,128]{1,0:T(8,128)(2,1)S(1)}, bf16[960,128]{1,0:T(8,128)(2,1)S(1)}, u32[]{:S(2)}, u32[]{:S(2)}) %collective-permute-start.10) | collective-permute-done | bytes 245792 | tf_op jit(solution)/shard_map/ppermute | solution.py:304
  130.0 0.7 copy.16
  130.7 0.0 all-to-all-done.2
  130.7 0.1 convert_reduce_fusion
  130.8 0.6 slice_bitcast_fusion.1
  131.4 0.7 copy.22
  (35 shorter events, 0.3 us)
Async XLA Ops:
  1.4 32.0 %copy-start.7 = (s32[1,2]{1,0:T(1,128)S(1)}, s32[1,2]{1,0:T(1,128)}, u32[]{:S(2)}) copy-start(s32[1,2]{1,0:T(1,128)} %constant.33.clone) | copy-start | bytes 28
  4.0 25.8 %collective-permute-start = (bf16[144,512]{1,0:T(8,128)(2,1)S(1)}, bf16[144,512]{1,0:T(8,128)(2,1)S(1)}, u32[]{:S(2)}, u32[]{:S(2)}) collective-permute-start(bf16[144,512]{1,0:T(8,128)(2,1)S(1)} %bitcast_dynamic-update-slice_fusion), channel_id=1, source_target_pairs={{0,4},{4,8},{8,12},{12,0},{1,5},{5,9},{9,13},{13,1},{2,6},{6,10},{... | collective-permute-start | bytes 442376 | tf_op jit(solution)/shard_map/ppermute | solution.py:240
  7.5 27.8 %collective-permute-start.1 = (bf16[144,512]{1,0:T(8,128)(2,1)S(1)}, bf16[144,512]{1,0:T(8,128)(2,1)S(1)}, u32[]{:S(2)}, u32[]{:S(2)}) collective-permute-start(bf16[144,512]{1,0:T(8,128)(2,1)S(1)} %bitcast_dynamic-update-slice_fusion), channel_id=1, source_target_pairs={{0,2},{2,0},{1,3},{3,1},{4,6},{6,4},{5,7},{7,5},{8,10},{10,8},{9,1... | collective-permute-start | bytes 442376 | tf_op jit(solution)/shard_map/ppermute | solution.py:253
  22.3 23.0 %collective-permute-start.7 = (bf16[144,512]{1,0:T(8,128)(2,1)S(1)}, bf16[144,512]{1,0:T(8,128)(2,1)S(1)}, u32[]{:S(2)}, u32[]{:S(2)}) collective-permute-start(bf16[144,512]{1,0:T(8,128)(2,1)S(1)} %bitcast_dynamic-update-slice_fusion), channel_id=1, source_target_pairs={{0,12},{4,0},{8,4},{12,8},{1,13},{5,1},{9,5},{13,9},{2,14},{6,2},{... | collective-permute-start | bytes 442376 | tf_op jit(solution)/shard_map/ppermute | solution.py:240
  25.9 19.4 %collective-permute-start.6 = (bf16[144,512]{1,0:T(8,128)(2,1)S(1)}, bf16[144,512]{1,0:T(8,128)(2,1)S(1)}, u32[]{:S(2)}, u32[]{:S(2)}) collective-permute-start(bf16[144,512]{1,0:T(8,128)(2,1)S(1)} %bitcast_dynamic-update-slice_fusion), channel_id=1, source_target_pairs={{0,8},{4,12},{8,0},{12,4},{1,9},{5,13},{9,1},{13,5},{2,10},{6,14},... | collective-permute-start | bytes 442376 | tf_op jit(solution)/shard_map/ppermute | solution.py:240
  29.8 30.9 %all-to-all-start = ((bf16[8,16,1280]{2,0,1:T(8,128)(2,1)}), bf16[8,16,1280]{2,0,1:T(8,128)(2,1)S(1)}, u32[]{:S(2)}, u32[]{:S(2)}) async-start(bf16[8,16,1280]{2,0,1:T(8,128)(2,1)} %bitcast.8), calls=%async_computation | async-start | bytes 655360 | tf_op jit(solution)/shard_map/all_to_all | solution.py:261
  35.3 12.1 %collective-permute-start.4 = (bf16[144,512]{1,0:T(8,128)(2,1)S(1)}, bf16[144,512]{1,0:T(8,128)(2,1)S(1)}, u32[]{:S(2)}, u32[]{:S(2)}) collective-permute-start(bf16[144,512]{1,0:T(8,128)(2,1)S(1)} %collective-permute-done.1), channel_id=1, source_target_pairs={{0,12},{4,0},{8,4},{12,8},{1,13},{5,1},{9,5},{13,9},{2,14},{6,2},{... | collective-permute-start | bytes 442376 | tf_op jit(solution)/shard_map/ppermute | solution.py:240
  38.9 10.4 %collective-permute-start.3 = (bf16[144,512]{1,0:T(8,128)(2,1)S(1)}, bf16[144,512]{1,0:T(8,128)(2,1)S(1)}, u32[]{:S(2)}, u32[]{:S(2)}) collective-permute-start(bf16[144,512]{1,0:T(8,128)(2,1)S(1)} %collective-permute-done.1), channel_id=1, source_target_pairs={{0,8},{4,12},{8,0},{12,4},{1,9},{5,13},{9,1},{13,5},{2,10},{6,14},... | collective-permute-start | bytes 442376 | tf_op jit(solution)/shard_map/ppermute | solution.py:240
  42.7 8.7 %collective-permute-start.2 = (bf16[144,512]{1,0:T(8,128)(2,1)S(1)}, bf16[144,512]{1,0:T(8,128)(2,1)S(1)}, u32[]{:S(2)}, u32[]{:S(2)}) collective-permute-start(bf16[144,512]{1,0:T(8,128)(2,1)S(1)} %collective-permute-done.1), channel_id=1, source_target_pairs={{0,4},{4,8},{8,12},{12,0},{1,5},{5,9},{9,13},{13,1},{2,6},{6,10},{... | collective-permute-start | bytes 442376 | tf_op jit(solution)/shard_map/ppermute | solution.py:240
  45.5 15.3 %copy-start.1 = (bf16[4,144,512]{2,1,0:T(8,128)(2,1)}, bf16[4,144,512]{2,1,0:T(8,128)(2,1)S(1)}, u32[]{:S(2)}) copy-start(bf16[4,144,512]{2,1,0:T(8,128)(2,1)S(1)} %pad_maximum_fusion.2.near_mine_hbm) | copy-start | bytes 1769476
  45.5 10.7 %collective-permute-start.8 = (bf16[4,144,512]{2,1,0:T(8,128)(2,1)S(1)}, bf16[4,144,512]{2,1,0:T(8,128)(2,1)S(1)}, u32[]{:S(2)}, u32[]{:S(2)}) collective-permute-start(bf16[4,144,512]{2,1,0:T(8,128)(2,1)S(1)} %pad_maximum_fusion.2.near_mine_hbm), channel_id=1, source_target_pairs={{0,1},{1,0},{2,3},{3,2},{4,5},{5,4},{6,7},{7,6},{8,9},{9,8},{10,11... | collective-permute-start | bytes 1769480 | tf_op jit(solution)/shard_map/ppermute | solution.py:262
  51.5 9.2 %copy-start.2 = (bf16[4,144,512]{2,1,0:T(8,128)(2,1)}, bf16[4,144,512]{2,1,0:T(8,128)(2,1)S(1)}, u32[]{:S(2)}) copy-start(bf16[4,144,512]{2,1,0:T(8,128)(2,1)S(1)} %pad_maximum_fusion.1.far_mine_hbm) | copy-start | bytes 1769476
  51.6 4.7 %collective-permute-start.5 = (bf16[4,144,512]{2,1,0:T(8,128)(2,1)S(1)}, bf16[4,144,512]{2,1,0:T(8,128)(2,1)S(1)}, u32[]{:S(2)}, u32[]{:S(2)}) collective-permute-start(bf16[4,144,512]{2,1,0:T(8,128)(2,1)S(1)} %pad_maximum_fusion.1.far_mine_hbm), channel_id=1, source_target_pairs={{0,1},{1,0},{2,3},{3,2},{4,5},{5,4},{6,7},{7,6},{8,9},{9,8},{10,11... | collective-permute-start | bytes 1769480 | tf_op jit(solution)/shard_map/ppermute | solution.py:264
  56.2 4.6 %copy-start.4 = (bf16[4,144,512]{2,1,0:T(8,128)(2,1)}, bf16[4,144,512]{2,1,0:T(8,128)(2,1)S(1)}, u32[]{:S(2)}) copy-start(bf16[4,144,512]{2,1,0:T(8,128)(2,1)S(1)} %collective-permute-done.8.near_other_hbm) | copy-start | bytes 1769476
  56.2 4.6 %copy-start.5 = (bf16[4,144,512]{2,1,0:T(8,128)(2,1)}, bf16[4,144,512]{2,1,0:T(8,128)(2,1)S(1)}, u32[]{:S(2)}) copy-start(bf16[4,144,512]{2,1,0:T(8,128)(2,1)S(1)} %collective-permute-done.5.far_other_hbm) | copy-start | bytes 1769476
  60.8 0.7 copy-start.3
  74.2 4.2 %collective-permute-start.9 = (bf16[4,672,128]{2,1,0:T(8,128)(2,1)}, bf16[4,672,128]{2,1,0:T(8,128)(2,1)S(1)}, u32[]{:S(2)}, u32[]{:S(2)}) collective-permute-start(bf16[4,672,128]{2,1,0:T(8,128)(2,1)} %get-tuple-element.19), channel_id=1, source_target_pairs={{0,1},{1,0},{2,3},{3,2},{4,5},{5,4},{6,7},{7,6},{8,9},{9,8},{10,11... | collective-permute-start | bytes 2064392 | tf_op jit(solution)/shard_map/ppermute | solution.py:293
  80.6 3.6 %copy-start.6 = (bf16[4,576,128]{2,1,0:T(8,128)(2,1)S(1)}, bf16[4,576,128]{2,1,0:T(8,128)(2,1)}, u32[]{:S(2)}) copy-start(bf16[4,576,128]{2,1,0:T(8,128)(2,1)} %get-tuple-element.23) | copy-start | bytes 1769476
  80.6 16.5 %all-to-all-start.1 = ((bf16[4,768,128]{2,1,0:T(8,128)(2,1)}), bf16[4,768,128]{2,1,0:T(8,128)(2,1)S(1)}, u32[]{:S(2)}, u32[]{:S(2)}) async-start(bf16[4,768,128]{2,1,0:T(8,128)(2,1)} %pad_maximum_fusion), calls=%async_computation.1 | async-start | bytes 1572864 | tf_op jit(solution)/shard_map/all_to_all | solution.py:299
  84.2 22.1 %collective-permute-start.11 = (bf16[4,576,128]{2,1,0:T(8,128)(2,1)S(1)}, bf16[4,576,128]{2,1,0:T(8,128)(2,1)S(1)}, u32[]{:S(2)}, u32[]{:S(2)}) collective-permute-start(bf16[4,576,128]{2,1,0:T(8,128)(2,1)S(1)} %copy-done.6), channel_id=1, source_target_pairs={{0,1},{1,0},{2,3},{3,2},{4,5},{5,4},{6,7},{7,6},{8,9},{9,8},{10,11... | collective-permute-start | bytes 1769480 | tf_op jit(solution)/shard_map/ppermute | solution.py:297
  97.1 9.3 %copy-start = (bf16[4,576,128]{2,1,0:T(8,128)(2,1)S(1)}, bf16[4,576,128]{2,1,0:T(8,128)(2,1)}, u32[]{:S(2)}) copy-start(bf16[4,576,128]{2,1,0:T(8,128)(2,1)} %get-tuple-element.22) | copy-start | bytes 1769476
  97.2 32.6 %collective-permute-start.10 = (bf16[960,128]{1,0:T(8,128)(2,1)S(1)}, bf16[960,128]{1,0:T(8,128)(2,1)S(1)}, u32[]{:S(2)}, u32[]{:S(2)}) collective-permute-start(bf16[960,128]{1,0:T(8,128)(2,1)S(1)} %pad_maximum_fusion.4), channel_id=1, source_target_pairs={{0,2},{2,0},{1,3},{3,1},{4,6},{6,4},{5,7},{7,5},{8,10},{10,8},{9,1... | collective-permute-start | bytes 737288 | tf_op jit(solution)/shard_map/ppermute | solution.py:304
  107.4 23.3 %all-to-all-start.2 = ((bf16[4,576,128]{2,1,0:T(8,128)(2,1)}), bf16[4,576,128]{2,1,0:T(8,128)(2,1)S(1)}, u32[]{:S(2)}, u32[]{:S(2)}) async-start(bf16[4,576,128]{2,1,0:T(8,128)(2,1)} %add_convert_fusion), calls=%async_computation.2 | async-start | bytes 1179648 | tf_op jit(solution)/shard_map/all_to_all | solution.py:306

commit v3 on v2

v3 whole, which is shorter than its diff:
```python
import math

import jax
import jax.numpy as jnp
from jax import lax
from jax.experimental import pallas as pl
from jax.experimental.pallas import tpu as pltpu
from jax.sharding import Mesh, PartitionSpec as P

NOPE = 128
ROPE = 64
VDIM = 128
LATENT = 512
LANES = 128
WIDTH = NOPE + ROPE
KEYED = LATENT + ROPE
N_Y, N_Z, N_C = 4, 2, 2
SWAP = [(0, 1), (1, 0)]
BF16 = jnp.bfloat16
F32 = jnp.float32
LOWEST = -1e29
HIDDEN = -1e30
EXPONENT = math.log2(math.e) * WIDTH ** (-0.5)
ORDER_FLOPS = 20_000_000_000
NEAR_FLOPS = 6_000_000_000


def dot(left, right, left_dim, right_dim):
    return lax.dot_general(
        left,
        right,
        (((left_dim,), (right_dim,)), ((), ())),
        preferred_element_type=F32,
    )


def unpack_keys(packed, keyed, base):
    block = packed.shape[1] * LATENT // KEYED
    folds = LATENT // LANES
    for j in range(N_Y):
        span = slice(base + j * block, base + (j + 1) * block)
        keyed[span, :LATENT] = packed[j, :block, :]
        rot = jnp.concatenate(
            [packed[j, block:, a * LANES : (a + 1) * LANES] for a in range(folds)], axis=0
        )
        keyed[span, LATENT:] = jnp.transpose(rot)


def forward_chunk(n, base, carry, bound_ref, rel, keyed, q_cat, o_lat, expo, dprob):
    top, total, delta = carry
    block = rel.shape[0]
    span = slice(base, base + N_Y * block)
    scores = dot(keyed[span, :], q_cat[...], 1, 1)
    dp = dot(keyed[span, :LATENT], o_lat[...], 1, 1)
    dprob[span, :] = dp
    visible = [rel[...] <= bound_ref[n * N_Y + j] for j in range(N_Y)]
    parts = [
        jnp.where(visible[j], scores[j * block : (j + 1) * block], HIDDEN)
        for j in range(N_Y)
    ]
    new_top = top
    for part in parts:
        new_top = jnp.maximum(new_top, jnp.max(part, axis=0, keepdims=True))
    keep = jnp.exp2((top - new_top) * EXPONENT)
    total = total * keep
    delta = delta * keep
    for j, part in enumerate(parts):
        e = jnp.exp2((part - new_top) * EXPONENT)
        expo[base + j * block : base + (j + 1) * block, :] = e
        total += jnp.sum(e, axis=0, keepdims=True)
        delta += jnp.sum(e * dp[j * block : (j + 1) * block], axis=0, keepdims=True)
    return new_top, total, delta


def set_relative(rel, count):
    rel[...] = lax.broadcasted_iota(jnp.int32, rel.shape, 0) - lax.rem(
        lax.broadcasted_iota(jnp.int32, rel.shape, 1), count
    )


def first_kernel(
    bound_ref,
    qg_hbm,
    wk_hbm,
    wv_hbm,
    keys_hbm,
    q_cat_hbm,
    o_lat_hbm,
    keyed_hbm,
    expo_hbm,
    dprob_hbm,
    stats_ref,
    qg_ref,
    wk_ref,
    wv_ref,
    packed,
    keyed,
    q_cat,
    o_lat,
    rel,
    expo,
    dprob,
    in_sem,
    out_sem,
):
    count = qg_ref.shape[0]
    heads = wk_ref.shape[1] // NOPE
    stacked = heads * count
    chunk = N_Y * rel.shape[0]
    loads = [
        pltpu.make_async_copy(qg_hbm, qg_ref, in_sem.at[0]),
        pltpu.make_async_copy(wk_hbm, wk_ref, in_sem.at[1]),
        pltpu.make_async_copy(wv_hbm, wv_ref, in_sem.at[2]),
        pltpu.make_async_copy(keys_hbm, packed, in_sem.at[3]),
    ]
    for load in loads:
        load.start()
    set_relative(rel, count)
    for load in loads:
        load.wait()
    for h in range(heads):
        rows = slice(h * count, (h + 1) * count)
        cols = slice(h * NOPE, (h + 1) * NOPE)
        plain = qg_ref[:, h * WIDTH : h * WIDTH + NOPE]
        grad = qg_ref[:, heads * WIDTH + h * VDIM : heads * WIDTH + (h + 1) * VDIM]
        q_cat[rows, :LATENT] = dot(plain, wk_ref[:, cols], 1, 1).astype(BF16)
        q_cat[rows, LATENT:] = qg_ref[:, h * WIDTH + NOPE : (h + 1) * WIDTH]
        o_lat[rows, :] = dot(grad, wv_ref[:, cols], 1, 1).astype(BF16)
    carry = (
        jnp.full((1, stacked), LOWEST, F32),
        jnp.zeros((1, stacked), F32),
        jnp.zeros((1, stacked), F32),
    )
    stores = [
        pltpu.make_async_copy(q_cat, q_cat_hbm, out_sem.at[0]),
        pltpu.make_async_copy(o_lat, o_lat_hbm, out_sem.at[1]),
    ]
    for store in stores:
        store.start()
    for n in range(N_Z):
        unpack_keys(packed.at[n], keyed, n * chunk)
        carry = forward_chunk(
            n, n * chunk, carry, bound_ref, rel, keyed, q_cat, o_lat, expo, dprob
        )
        span = pl.ds(n * chunk, chunk)
        for i, (mine, out) in enumerate(
            ((keyed, keyed_hbm), (expo, expo_hbm), (dprob, dprob_hbm))
        ):
            store = pltpu.make_async_copy(
                mine.at[span], out.at[span], out_sem.at[2 + 3 * n + i]
            )
            store.start()
            stores.append(store)
        stats_ref[n : n + 1, :] = carry[0]
    stats_ref[N_Z : N_Z + 1, :] = carry[1]
    stats_ref[N_Z + 1 : N_Z + 2, :] = carry[2]
    for store in stores:
        store.wait()


def second_kernel(
    bound_ref,
    row_ref,
    slot_ref,
    stats_ref,
    q_cat_hbm,
    o_lat_hbm,
    wk_hbm,
    keys_hbm,
    keyed_hbm,
    expo_hbm,
    dprob_hbm,
    d_far_other_hbm,
    d_far_mine_hbm,
    d_near_other_hbm,
    d_near_mine_hbm,
    wk_ref,
    packed,
    keyed,
    d_near,
    d_far,
    dq_ref,
    q_cat,
    o_lat,
    rel,
    expo,
    dprob,
    in_sem,
    out_sem,
):
    scale = WIDTH ** (-0.5)
    heads = wk_ref.shape[1] // NOPE
    stacked = q_cat.shape[0]
    count = stacked // heads
    block = rel.shape[0]
    chunk = N_Y * block
    half = N_Z * chunk
    folds = LATENT // LANES
    slab = folds * block + ROPE
    late = pl.ds(half, half)
    loads = [
        pltpu.make_async_copy(keys_hbm, packed, in_sem.at[0]),
        pltpu.make_async_copy(q_cat_hbm, q_cat, in_sem.at[1]),
        pltpu.make_async_copy(o_lat_hbm, o_lat, in_sem.at[2]),
        pltpu.make_async_copy(keyed_hbm, keyed.at[late], in_sem.at[3]),
        pltpu.make_async_copy(expo_hbm, expo.at[late], in_sem.at[4]),
        pltpu.make_async_copy(dprob_hbm, dprob.at[late], in_sem.at[5]),
        pltpu.make_async_copy(wk_hbm, wk_ref, in_sem.at[6]),
    ]
    for load in loads:
        load.start()
    set_relative(rel, count)
    for load in loads[:3]:
        load.wait()
    carry = (
        stats_ref[N_Z - 1 : N_Z, :],
        stats_ref[N_Z : N_Z + 1, :],
        stats_ref[N_Z + 1 : N_Z + 2, :],
    )
    tops = []
    for n in range(N_Z):
        unpack_keys(packed.at[n], keyed, n * chunk)
        carry = forward_chunk(
            n, n * chunk, carry, bound_ref, rel, keyed, q_cat, o_lat, expo, dprob
        )
        tops.append(carry[0])
    tops += [stats_ref[n : n + 1, :] for n in range(N_Z)]
    for load in loads[3:]:
        load.wait()
    top, total, delta = carry
    inverse = 1.0 / total
    delta = delta * inverse
    dq_lat = jnp.zeros((stacked, KEYED), F32)
    stores = []
    for m in (0, 2, 1, 3):
        z_slot, c_slot = m % N_Z, m // N_Z
        span = slice(m * chunk, (m + 1) * chunk)
        probs = expo[span, :] * (jnp.exp2((tops[m] - top) * EXPONENT) * inverse)
        dscore = (probs * (dprob[span, :] - delta) * scale).astype(BF16)
        probs_low = probs.astype(BF16)
        d_key = dot(dscore, q_cat[...], 1, 0)
        d_lat = (d_key[:, :LATENT] + dot(probs_low, o_lat[...], 1, 0)).astype(BF16)
        d_rot = d_key[:, LATENT:].astype(BF16)
        for j in range(N_Y):
            rows = slice(j * block, (j + 1) * block)
            place = (d_far, d_near)[z_slot].at[c_slot, slot_ref[j]]
            for a in range(folds):
                place[a * block : (a + 1) * block, :] = d_lat[
                    rows, a * LANES : (a + 1) * LANES
                ]
            place[folds * block : slab, :] = jnp.transpose(d_rot[rows])
        if z_slot == 0:
            store = pltpu.make_async_copy(
                d_far.at[c_slot],
                (d_far_other_hbm, d_far_mine_hbm)[c_slot],
                out_sem.at[c_slot],
            )
            store.start()
            stores.append(store)
        dq_lat += dot(dscore, keyed[span, :], 0, 0)
    dq_low = dq_lat.astype(BF16)
    for h in range(heads):
        rows = slice(h * count, (h + 1) * count)
        cols = slice(h * NOPE, (h + 1) * NOPE)
        dq_ref[:, h * WIDTH : h * WIDTH + NOPE] = dot(
            dq_low[rows, :LATENT], wk_ref[:, cols], 1, 0
        )
        dq_ref[:, h * WIDTH + NOPE : (h + 1) * WIDTH] = dq_lat[rows, LATENT:]
    few = count // (N_Y * N_Z * N_C)
    for n in range(N_C):
        for j in range(N_Y):
            pieces = []
            for dz in range(N_Z):
                start = pl.multiple_of(row_ref[(n * N_Y + j) * N_Z + dz], few)
                for a in range(heads * WIDTH // LANES):
                    pieces.append(dq_ref[pl.ds(start, few), a * LANES : (a + 1) * LANES])
            d_near[n, j, slab:, :] = jnp.concatenate(pieces, axis=0).astype(BF16)
        store = pltpu.make_async_copy(
            d_near.at[n], (d_near_other_hbm, d_near_mine_hbm)[n], out_sem.at[N_C + n]
        )
        store.start()
        stores.append(store)
    for store in stores:
        store.wait()


def attention(bounds_mine, bounds_other, starts, slots, qg, w_key, w_value, mine, other):
    count = qg.shape[0]
    heads = w_key.shape[1] // NOPE
    stacked = heads * count
    tall = mine.shape[2]
    block = tall * LATENT // KEYED
    half = N_Z * N_Y * block
    slab = block * KEYED // LANES
    extra = N_Z * (count // (N_Y * N_Z * N_C)) * heads * WIDTH // LANES
    near_slab = slab + extra
    hbm = pl.BlockSpec(memory_space=pl.ANY)
    smem = pl.BlockSpec(memory_space=pltpu.SMEM)
    vmem = pl.BlockSpec(memory_space=pltpu.VMEM)
    middle = [
        jax.ShapeDtypeStruct((stacked, KEYED), BF16),
        jax.ShapeDtypeStruct((stacked, LATENT), BF16),
        jax.ShapeDtypeStruct((half, KEYED), BF16),
        jax.ShapeDtypeStruct((half, stacked), F32),
        jax.ShapeDtypeStruct((half, stacked), F32),
        jax.ShapeDtypeStruct((8, stacked), F32),
    ]
    q_cat, o_lat, keyed, expo, dprob, stats = pl.pallas_call(
        first_kernel,
        out_shape=middle,
        in_specs=[smem] + [hbm] * 4,
        out_specs=[hbm] * 5 + [vmem],
        scratch_shapes=[
            pltpu.VMEM(qg.shape, BF16),
            pltpu.VMEM(w_key.shape, BF16),
            pltpu.VMEM(w_value.shape, BF16),
            pltpu.VMEM(mine.shape, BF16),
            pltpu.VMEM((half, KEYED), BF16),
            pltpu.VMEM((stacked, KEYED), BF16),
            pltpu.VMEM((stacked, LATENT), BF16),
            pltpu.VMEM((block, stacked), jnp.int32),
            pltpu.VMEM((half, stacked), F32),
            pltpu.VMEM((half, stacked), F32),
            pltpu.SemaphoreType.DMA((4,)),
            pltpu.SemaphoreType.DMA((2 + 3 * N_Z,)),
        ],
        compiler_params=pltpu.CompilerParams(vmem_limit_bytes=56 * 2**20),
        cost_estimate=pl.CostEstimate(
            flops=ORDER_FLOPS, bytes_accessed=12 * half * stacked, transcendentals=half * stacked
        ),
    )(bounds_mine, qg, w_key, w_value, mine)
    return pl.pallas_call(
        second_kernel,
        out_shape=[jax.ShapeDtypeStruct((N_Y, slab, LANES), BF16)] * N_C
        + [jax.ShapeDtypeStruct((N_Y, near_slab, LANES), BF16)] * N_C,
        in_specs=[smem] * 3 + [vmem] + [hbm] * 7,
        out_specs=[hbm] * 4,
        scratch_shapes=[
            pltpu.VMEM(w_key.shape, BF16),
            pltpu.VMEM(other.shape, BF16),
            pltpu.VMEM((2 * half, KEYED), BF16),
            pltpu.VMEM((N_C, N_Y, near_slab, LANES), BF16),
            pltpu.VMEM((N_C, N_Y, slab, LANES), BF16),
            pltpu.VMEM((count, heads * WIDTH), F32),
            pltpu.VMEM((stacked, KEYED), BF16),
            pltpu.VMEM((stacked, LATENT), BF16),
            pltpu.VMEM((block, stacked), jnp.int32),
            pltpu.VMEM((2 * half, stacked), F32),
            pltpu.VMEM((2 * half, stacked), F32),
            pltpu.SemaphoreType.DMA((7,)),
            pltpu.SemaphoreType.DMA((2 * N_C,)),
        ],
        compiler_params=pltpu.CompilerParams(vmem_limit_bytes=56 * 2**20),
        cost_estimate=pl.CostEstimate(
            flops=2 * half * stacked * (5 * KEYED + 3 * LATENT),
            bytes_accessed=16 * half * stacked,
            transcendentals=half * stacked,
        ),
    )(bounds_other, starts, slots, stats, q_cat, o_lat, w_key, other, keyed, expo, dprob)


def payload_kernel(mine_ref, got_ref, dq_ref, out_ref):
    piece = dq_ref.shape[2]
    slab = mine_ref.shape[1] - N_Z * piece
    own = slice(slab + piece, slab + N_Z * piece)
    for j in range(N_Y):
        out_ref[j, :slab, :] = (
            mine_ref[j, :slab, :].astype(F32) + got_ref[j, :slab, :].astype(F32)
        ).astype(BF16)
        parts = (mine_ref[j, own, :], got_ref[j, own, :], dq_ref[j, 0], dq_ref[j, 1])
        for i, part in enumerate(parts):
            out_ref[j, slab + i * piece : slab + (i + 1) * piece, :] = part


def near_payload(mine, got, dq):
    tall = mine.shape[1] + dq.shape[1] * dq.shape[2]
    vmem = pl.BlockSpec(memory_space=pltpu.VMEM)
    return pl.pallas_call(
        payload_kernel,
        out_shape=jax.ShapeDtypeStruct((N_Y, tall, LANES), BF16),
        in_specs=[vmem] * 3,
        out_specs=vmem,
        cost_estimate=pl.CostEstimate(
            flops=NEAR_FLOPS, bytes_accessed=6 * mine.size, transcendentals=0
        ),
    )(mine, got, dq)


def unpack_kernel(packed_ref, latent_ref, rope_ref):
    block = latent_ref.shape[0]
    for a in range(LATENT // LANES):
        latent_ref[:, a * LANES : (a + 1) * LANES] = packed_ref[a * block : (a + 1) * block, :]
    rope_ref[...] = packed_ref[LATENT // LANES * block :, :]


def unpack(packed):
    block = packed.shape[0] * LANES // KEYED
    vmem = pl.BlockSpec(memory_space=pltpu.VMEM)
    return pl.pallas_call(
        unpack_kernel,
        out_shape=[
            jax.ShapeDtypeStruct((block, LATENT), BF16),
            jax.ShapeDtypeStruct((ROPE, LANES), BF16),
        ],
        in_specs=[vmem],
        out_specs=[vmem] * 2,
        cost_estimate=pl.CostEstimate(
            flops=ORDER_FLOPS, bytes_accessed=4 * packed.size, transcendentals=0
        ),
    )(packed)


def shift(block, by):
    return lax.ppermute(block, "y", [(i, (i + by) % N_Y) for i in range(N_Y)])


def on_device(query, grad_out, latent, rope_key, w_key, w_value, offset):
    few = query.shape[0]
    n_sp = N_Y * N_Z * N_C
    block = latent.shape[0]
    folds = LATENT // LANES
    y, z, c = lax.axis_index("y"), lax.axis_index("z"), lax.axis_index("c")
    turned = rope_key.T.reshape(folds, ROPE // folds, block)
    pack = jnp.concatenate(
        [latent, jnp.transpose(turned, (1, 0, 2)).reshape(-1, LATENT)], axis=0
    )
    far = lax.ppermute(pack, "z", SWAP)
    qg = jnp.concatenate(
        [query.reshape(few, n_sp, -1), grad_out.reshape(few, n_sp, -1)], axis=2
    ).reshape(few, -1)
    qg, pack = lax.optimization_barrier((qg, pack))
    qg = lax.all_to_all(qg, ("y", "z", "c"), split_axis=1, concat_axis=0, tiled=True)
    both = jnp.stack([far, pack])
    mine = jnp.stack([both] + [shift(both, s) for s in range(1, N_Y)], axis=1)
    other = lax.ppermute(mine, "c", SWAP)

    steps = jnp.arange(N_Y, dtype=jnp.int32)

    def owner(y_of, z_of, c_of):
        return ((y_of * N_Z + z_of) * N_C + c_of).astype(jnp.int32)

    shifted = lax.rem(y - steps + N_Y, N_Y)
    owners = [
        jnp.concatenate([owner(shifted, z ^ dz, c_of) for dz in (1, 0)])
        for c_of in (c, c ^ 1)
    ]
    bounds_mine, bounds_other = (offset[0] - of * block for of in owners)
    starts = jnp.stack(
        [
            owner(steps[:, None], z ^ jnp.array([[1, 0]]), c ^ dc).reshape(-1)
            for dc in (1, 0)
        ]
    ).reshape(-1)
    d_other, d_mine, d_near_other, d_near_mine = attention(
        bounds_mine,
        bounds_other,
        starts * few,
        shifted.astype(jnp.int32),
        qg,
        w_key,
        w_value,
        mine,
        other,
    )
    slab = d_mine.shape[1]
    got = lax.ppermute(d_other, "c", SWAP)
    sent = (d_mine.astype(F32) + got.astype(F32)).astype(BF16)
    sent, d_near_other = lax.optimization_barrier((sent, d_near_other))
    near_got = lax.ppermute(d_near_other, "c", SWAP)
    piece = (d_near_mine.shape[1] - slab) // N_Z
    pieces = [d_near_mine[:, slab:], near_got[:, slab:]]
    dq_got = lax.ppermute(jnp.stack([p[:, :piece] for p in pieces], axis=1), "z", SWAP)
    slots = lax.all_to_all(sent, "y", split_axis=0, concat_axis=0, tiled=True)
    leaving = jnp.sum(slots.astype(F32), axis=0).astype(BF16)
    back = lax.ppermute(leaving, "z", SWAP)
    near = near_payload(d_near_mine, near_got, dq_got)
    near = lax.all_to_all(near, "y", split_axis=0, concat_axis=0, tiled=True)
    near_sum = jnp.sum(near[:, :slab].astype(F32), axis=0)
    back_latent, back_rope = unpack(back)
    near_latent = jnp.transpose(
        near_sum[: folds * block].reshape(folds, block, LANES), (1, 0, 2)
    ).reshape(block, LATENT)
    d_latent = (near_latent + back_latent.astype(F32)).astype(BF16)
    d_rope_key = (near_sum[folds * block :] + back_rope.astype(F32)).astype(BF16).T
    dq = near[:, slab:].reshape(N_Y, N_Z, N_C, -1, few, LANES)
    dq = jnp.where(z == 1, dq[:, ::-1], dq)
    dq = jnp.where(c == 1, dq[:, :, ::-1], dq)
    d_query = jnp.transpose(dq, (4, 0, 1, 2, 3, 5)).reshape(few, -1)
    return (d_query, d_latent, d_rope_key)


def solution(mesh):
    parts = mesh.devices.shape[0]
    split = Mesh(mesh.devices.reshape(parts, N_Y, N_Z, N_C), ("dp", "y", "z", "c"))
    rows = P(("dp", "y", "z", "c"), None)
    columns = P(None, ("y", "z", "c"))
    return jax.shard_map(
        on_device,
        mesh=split,
        in_specs=(rows, rows, rows, rows, columns, columns, P("dp")),
        out_specs=(rows, rows, rows),
        check_vma=False,
    )
```

time: 133 us -> 131 us (0.985)
  the two profiles are of different devices: /device:TPU:32 before, /device:TPU:38 now
where the time goes in v3:
time: 131 us; the launch traced here: 130 us
  starting transfers between devices  69.6 us (53%)
  waiting for transfers between devices  23.9 us (18%)
  Pallas kernels  20.8 us (16%)
  other arithmetic  8.23 us (6%)
  local copies, waits for them, and re-layouts  6.33 us (5%)
  between operations  1.59 us (1%)
    ppermute x1, starting transfers between devices, on_device(): far = lax.ppermute(pack, 'z', SWAP)  14.8 us
    ppermute x1, starting transfers between devices, on_device(): lax.ppermute(jnp.stack([p[:, :piece] for p in pieces], axis=1), 'z', SWAP)  13.4 us
    ppermute x3, starting transfers between devices, shift(): return lax.ppermute(block, 'y', [(i, (i + by) % N_Y) for i in range(N_Y)])  11.9 us
    pallas_call x1, Pallas kernels, attention(): pl.pallas_call(second_kernel, out_shape=[jax.ShapeDtypeStruct((N_Y, slab,...  10.4 us
    ppermute x1, waiting for transfers between devices, on_device(): far = lax.ppermute(pack, 'z', SWAP)  10 us
    ppermute x1, starting transfers between devices, on_device(): back = lax.ppermute(leaving, 'z', SWAP)  9.61 us
    pallas_call x1, Pallas kernels, attention(): pl.pallas_call(first_kernel, out_shape=middle, in_specs=[smem] + [hbm] *...  6.43 us
    ppermute x1, waiting for transfers between devices, on_device(): back = lax.ppermute(leaving, 'z', SWAP)  6.36 us
  transfers between devices with their start and end apart: 12, of which 6 were waited for; matrix products, arithmetic and copies ran while one was open for 4% of the time, Pallas kernels for 8%

profile of v3, /device:TPU:38, one launch (start us, length us, event | category | flops | bytes accessed | tf_op | source)
XLA Modules:
  0.0 130.4 jit_solution(1807570562885211688)
XLA Ops:
  0.6 0.0 copy-start.9
  0.6 0.7 copy.17
  1.4 0.9 constant_dynamic-update-slice_fusion
  2.3 14.8 %collective-permute-start = (bf16[144,512]{1,0:T(8,128)(2,1)S(1)}, bf16[144,512]{1,0:T(8,128)(2,1)S(1)}, u32[]{:S(2)}, u32[]{:S(2)}) collective-permute-start(bf16[144,512]{1,0:T(8,128)(2,1)S(1)} %bitcast_dynamic-update-slice_fusion), channel_id=1, source_target_pairs={{0,2},{2,0},{1,3},{3,1},{4,6},{6,4},{5,7},{7,5},{8,10},{10,8},{9,1... | collective-permute-start | bytes 442376 | tf_op jit(solution)/shard_map/ppermute | solution.py:427
  17.1 1.7 %pad_maximum_fusion.1 = bf16[8,16,1280]{2,0,1:T(8,128)(2,1)} fusion(bf16[8,16,512]{2,0,1:T(8,128)(2,1)} %bitcast.60, bf16[8,16,768]{2,0,1:T(8,128)(2,1)} %bitcast.58), kind=kLoop, calls=%fused_computation.3 | loop fusion | flops 655360 | bytes 655360 | tf_op jit(solution)/shard_map/concatenate | solution.py:428
  18.9 4.6 %all-to-all-start = ((bf16[8,16,1280]{2,0,1:T(8,128)(2,1)}), bf16[8,16,1280]{2,0,1:T(8,128)(2,1)S(1)}, u32[]{:S(2)}, u32[]{:S(2)}) async-start(bf16[8,16,1280]{2,0,1:T(8,128)(2,1)} %bitcast.8), calls=%async_computation | async-start | bytes 655360 | tf_op jit(solution)/shard_map/all_to_all | solution.py:432
  23.5 0.1 fusion.4
  23.6 0.1 add.140
  23.7 0.1 add.146
  23.8 0.6 compare_select_fusion.slot_ref
  25.0 0.6 mul.66.row_ref
  25.6 10.0 %collective-permute-done = bf16[144,512]{1,0:T(8,128)(2,1)S(1)} collective-permute-done((bf16[144,512]{1,0:T(8,128)(2,1)S(1)}, bf16[144,512]{1,0:T(8,128)(2,1)S(1)}, u32[]{:S(2)}, u32[]{:S(2)}) %collective-permute-start) | collective-permute-done | bytes 147488 | tf_op jit(solution)/shard_map/ppermute | solution.py:427
  35.7 4.9 %collective-permute-start.2 = (bf16[2,144,512]{2,1,0:T(8,128)(2,1)S(1)}, bf16[2,144,512]{2,1,0:T(8,128)(2,1)S(1)}, u32[]{:S(2)}, u32[]{:S(2)}) collective-permute-start(bf16[2,144,512]{2,1,0:T(8,128)(2,1)S(1)} %get-tuple-element.36), channel_id=1, source_target_pairs={{0,8},{4,12},{8,0},{12,4},{1,9},{5,13},{9,1},{13,5},{2,10},{6,14},... | collective-permute-start | bytes 884744 | tf_op jit(solution)/shard_map/ppermute | solution.py:414
  40.5 2.5 %collective-permute-start.1 = (bf16[2,144,512]{2,1,0:T(8,128)(2,1)S(1)}, bf16[2,144,512]{2,1,0:T(8,128)(2,1)S(1)}, u32[]{:S(2)}, u32[]{:S(2)}) collective-permute-start(bf16[2,144,512]{2,1,0:T(8,128)(2,1)S(1)} %get-tuple-element.36), channel_id=1, source_target_pairs={{0,4},{4,8},{8,12},{12,0},{1,5},{5,9},{9,13},{13,1},{2,6},{6,10},{... | collective-permute-start | bytes 884744 | tf_op jit(solution)/shard_map/ppermute | solution.py:414
  43.0 4.6 %collective-permute-start.3 = (bf16[2,144,512]{2,1,0:T(8,128)(2,1)S(1)}, bf16[2,144,512]{2,1,0:T(8,128)(2,1)S(1)}, u32[]{:S(2)}, u32[]{:S(2)}) collective-permute-start(bf16[2,144,512]{2,1,0:T(8,128)(2,1)S(1)} %get-tuple-element.36), channel_id=1, source_target_pairs={{0,12},{4,0},{8,4},{12,8},{1,13},{5,1},{9,5},{13,9},{2,14},{6,2},{... | collective-permute-start | bytes 884744 | tf_op jit(solution)/shard_map/ppermute | solution.py:414
  47.6 0.7 fusion.7.bound_ref
  48.3 0.6 fusion.6.bound_ref
  48.9 0.0 collective-permute-done.2
  48.9 1.7 %collective-permute-done.1 = bf16[2,144,512]{2,1,0:T(8,128)(2,1)S(1)} collective-permute-done((bf16[2,144,512]{2,1,0:T(8,128)(2,1)S(1)}, bf16[2,144,512]{2,1,0:T(8,128)(2,1)S(1)}, u32[]{:S(2)}, u32[]{:S(2)}) %collective-permute-start.1) | collective-permute-done | bytes 294944 | tf_op jit(solution)/shard_map/ppermute | solution.py:414
  50.6 1.2 collective-permute-done.3
  51.8 0.1 pad_maximum_fusion.keys_hbm
  52.0 1.9 %collective-permute-start.4 = (bf16[2,4,144,512]{3,2,1,0:T(8,128)(2,1)S(1)}, bf16[2,4,144,512]{3,2,1,0:T(8,128)(2,1)S(1)}, u32[]{:S(2)}, u32[]{:S(2)}) collective-permute-start(bf16[2,4,144,512]{3,2,1,0:T(8,128)(2,1)S(1)} %pad_maximum_fusion.keys_hbm), channel_id=1, source_target_pairs={{0,1},{1,0},{2,3},{3,2},{4,5},{5,4},{6,7},{7,6},{8,9},{9,8},{10,11... | collective-permute-start | bytes 3538952 | tf_op jit(solution)/shard_map/ppermute | solution.py:435
  53.9 0.0 all-to-all-done
  54.0 0.7 copy-done.1
  54.7 6.4 %shard_map.112 = (bf16[512,576]{1,0:T(8,128)(2,1)}, bf16[512,512]{1,0:T(8,128)(2,1)}, bf16[1024,576]{1,0:T(8,128)(2,1)}, f32[1024,512]{1,0:T(8,128)}, f32[1024,512]{1,0:T(8,128)}, /*index=5*/f32[8,512]{1,0:T(8,128)}) custom-call(s32[8]{0:T(128)} %fusion.7.bound_ref, bf16[128,1280]{1,0:T(8,128)(2,1)} %bitcast.53, bf16[512,512]{1,0:T(8,128)(2,1)} %wk_hbm.3, ...), custom_call_target="tpu_custom_call" | custom-call | flops 20000000000 | bytes 6291456 | tf_op jit(solution)/shard_map/pallas_call | solution.py:308
  61.1 1.0 copy-done.5
  62.2 10.4 %shard_map.113 = (bf16[4,576,128]{2,1,0:T(8,128)(2,1)}, bf16[4,576,128]{2,1,0:T(8,128)(2,1)}, bf16[4,672,128]{2,1,0:T(8,128)(2,1)}, bf16[4,672,128]{2,1,0:T(8,128)(2,1)}) custom-call(s32[8]{0:T(128)} %fusion.6.bound_ref, s32[16]{0:T(128)} %mul.66.row_ref, s32[4]{0:T(128)} %compare_select_fusion.slot_ref, f32[8,512]{1,0:T(8,128)} %get-tuple-element.21.stats_ref, ...), custom_call_target="tpu_custom_call" | custom-call | flops 4630511616 | bytes 8388608 | tf_op jit(solution)/shard_map/pallas_call | solution.py:332
  72.6 2.5 %collective-permute-start.5 = (bf16[4,576,128]{2,1,0:T(8,128)(2,1)}, bf16[4,576,128]{2,1,0:T(8,128)(2,1)S(1)}, u32[]{:S(2)}, u32[]{:S(2)}) collective-permute-start(bf16[4,576,128]{2,1,0:T(8,128)(2,1)} %get-tuple-element.29), channel_id=1, source_target_pairs={{0,1},{1,0},{2,3},{3,2},{4,5},{5,4},{6,7},{7,6},{8,9},{9,8},{10,11... | collective-permute-start | bytes 1769480 | tf_op jit(solution)/shard_map/ppermute | solution.py:466
  75.1 1.8 %collective-permute-done.5 = bf16[4,576,128]{2,1,0:T(8,128)(2,1)S(1)} collective-permute-done((bf16[4,576,128]{2,1,0:T(8,128)(2,1)}, bf16[4,576,128]{2,1,0:T(8,128)(2,1)S(1)}, u32[]{:S(2)}, u32[]{:S(2)}) %collective-permute-start.5) | collective-permute-done | bytes 589856 | tf_op jit(solution)/shard_map/ppermute | solution.py:466
  77.0 2.1 %add_convert_fusion = bf16[4,576,128]{2,1,0:T(8,128)(2,1)} fusion(bf16[4,576,128]{2,1,0:T(8,128)(2,1)S(1)} %collective-permute-done.5, bf16[4,576,128]{2,1,0:T(8,128)(2,1)} %get-tuple-element.28), kind=kLoop, calls=%fused_computation.2 | loop fusion | flops 1179648 | bytes 1769472 | tf_op jit(solution)/shard_map/convert_element_type | solution.py:467
  79.0 2.3 %collective-permute-start.6 = (bf16[4,672,128]{2,1,0:T(8,128)(2,1)S(1)}, bf16[4,672,128]{2,1,0:T(8,128)(2,1)S(1)}, u32[]{:S(2)}, u32[]{:S(2)}) collective-permute-start(bf16[4,672,128]{2,1,0:T(8,128)(2,1)S(1)} %copy-done.6), channel_id=1, source_target_pairs={{0,1},{1,0},{2,3},{3,2},{4,5},{5,4},{6,7},{7,6},{8,9},{9,8},{10,11... | collective-permute-start | bytes 2064392 | tf_op jit(solution)/shard_map/ppermute | solution.py:469
  81.3 5.0 %all-to-all-start.2 = ((bf16[4,576,128]{2,1,0:T(8,128)(2,1)}), bf16[4,576,128]{2,1,0:T(8,128)(2,1)S(1)}, u32[]{:S(2)}, u32[]{:S(2)}) async-start(bf16[4,576,128]{2,1,0:T(8,128)(2,1)} %add_convert_fusion), calls=%async_computation.2 | async-start | bytes 1179648 | tf_op jit(solution)/shard_map/all_to_all | solution.py:473
  86.3 0.8 slice_bitcast_fusion.1
  87.1 13.4 %collective-permute-start.7 = (bf16[4,2,48,128]{3,2,1,0:T(8,128)(2,1)S(1)}, bf16[4,2,48,128]{3,2,1,0:T(8,128)(2,1)S(1)}, u32[]{:S(2)}, u32[]{:S(2)}) collective-permute-start(bf16[4,2,48,128]{3,2,1,0:T(8,128)(2,1)S(1)} %pad_maximum_fusion.3), channel_id=1, source_target_pairs={{0,2},{2,0},{1,3},{3,1},{4,6},{6,4},{5,7},{7,5},{8,10},{10,8},{9,1... | collective-permute-start | bytes 294920 | tf_op jit(solution)/shard_map/ppermute | solution.py:472
  100.6 0.1 reduce_sum.22
  100.7 9.6 %collective-permute-start.8 = (bf16[576,128]{1,0:T(8,128)(2,1)S(1)}, bf16[576,128]{1,0:T(8,128)(2,1)S(1)}, u32[]{:S(2)}, u32[]{:S(2)}) collective-permute-start(bf16[576,128]{1,0:T(8,128)(2,1)S(1)} %reduce_sum.22), channel_id=1, source_target_pairs={{0,2},{2,0},{1,3},{3,1},{4,6},{6,4},{5,7},{7,5},{8,10},{10,8},{9,1... | collective-permute-start | bytes 442376 | tf_op jit(solution)/shard_map/ppermute | solution.py:475
  110.3 0.0 copy-start.8
  110.3 0.6 copy-done.8
  111.0 2.3 %shard_map.114 = bf16[4,768,128]{2,1,0:T(8,128)(2,1)} custom-call(bf16[4,672,128]{2,1,0:T(8,128)(2,1)} %get-tuple-element.27.mine_ref, bf16[4,672,128]{2,1,0:T(8,128)(2,1)} %copy-done.4, bf16[4,2,48,128]{3,2,1,0:T(8,128)(2,1)} %copy-done.8), custom_call_target="tpu_custom_call" | custom-call | flops 6000000000 | bytes 2064384 | tf_op jit(solution)/shard_map/pallas_call | solution.py:378
  113.3 3.5 %all-to-all-start.1 = ((bf16[4,768,128]{2,1,0:T(8,128)(2,1)}), bf16[4,768,128]{2,1,0:T(8,128)(2,1)S(1)}, u32[]{:S(2)}, u32[]{:S(2)}) async-start(bf16[4,768,128]{2,1,0:T(8,128)(2,1)} %shard_map.114), calls=%async_computation.1 | async-start | bytes 1572864 | tf_op jit(solution)/shard_map/all_to_all | solution.py:477
  116.8 6.4 %collective-permute-done.8.packed_ref = bf16[576,128]{1,0:T(8,128)(2,1)S(1)} collective-permute-done((bf16[576,128]{1,0:T(8,128)(2,1)S(1)}, bf16[576,128]{1,0:T(8,128)(2,1)S(1)}, u32[]{:S(2)}, u32[]{:S(2)}) %collective-permute-start.8) | collective-permute-done | bytes 147488 | tf_op jit(solution)/shard_map/ppermute | solution.py:475
  123.2 0.7 copy-done.7
  123.8 1.6 %shard_map.115 = (bf16[128,512]{1,0:T(8,128)(2,1)}, bf16[64,128]{1,0:T(8,128)(2,1)}) custom-call(bf16[576,128]{1,0:T(8,128)(2,1)} %copy-done.7), custom_call_target="tpu_custom_call" | custom-call | flops 20000000000 | bytes 294912 | tf_op jit(solution)/shard_map/pallas_call | solution.py:399
  125.4 2.8 %all-to-all-done.1 = bf16[4,768,128]{2,1,0:T(8,128)(2,1)S(1)} async-done(((bf16[4,768,128]{2,1,0:T(8,128)(2,1)}), bf16[4,768,128]{2,1,0:T(8,128)(2,1)S(1)}, u32[]{:S(2)}, u32[]{:S(2)}) %all-to-all-start.1) | async-done | bytes 786464 | tf_op jit(solution)/shard_map/all_to_all | solution.py:477
  128.2 0.1 convert_reduce_fusion
  128.3 0.6 fusion.2
  128.9 0.7 fusion
  129.7 0.7 reverse_select_fusion
  (30 shorter events, 0.2 us)
Async XLA Ops:
  0.6 22.8 %copy-start.9 = (s32[1,2]{1,0:T(1,128)S(1)}, s32[1,2]{1,0:T(1,128)}, u32[]{:S(2)}) copy-start(s32[1,2]{1,0:T(1,128)} %constant.33.clone) | copy-start | bytes 28
  2.3 33.3 %collective-permute-start = (bf16[144,512]{1,0:T(8,128)(2,1)S(1)}, bf16[144,512]{1,0:T(8,128)(2,1)S(1)}, u32[]{:S(2)}, u32[]{:S(2)}) collective-permute-start(bf16[144,512]{1,0:T(8,128)(2,1)S(1)} %bitcast_dynamic-update-slice_fusion), channel_id=1, source_target_pairs={{0,2},{2,0},{1,3},{3,1},{4,6},{6,4},{5,7},{7,5},{8,10},{10,8},{9,1... | collective-permute-start | bytes 442376 | tf_op jit(solution)/shard_map/ppermute | solution.py:427
  18.9 35.0 %all-to-all-start = ((bf16[8,16,1280]{2,0,1:T(8,128)(2,1)}), bf16[8,16,1280]{2,0,1:T(8,128)(2,1)S(1)}, u32[]{:S(2)}, u32[]{:S(2)}) async-start(bf16[8,16,1280]{2,0,1:T(8,128)(2,1)} %bitcast.8), calls=%async_computation | async-start | bytes 655360 | tf_op jit(solution)/shard_map/all_to_all | solution.py:432
  35.7 13.2 %collective-permute-start.2 = (bf16[2,144,512]{2,1,0:T(8,128)(2,1)S(1)}, bf16[2,144,512]{2,1,0:T(8,128)(2,1)S(1)}, u32[]{:S(2)}, u32[]{:S(2)}) collective-permute-start(bf16[2,144,512]{2,1,0:T(8,128)(2,1)S(1)} %get-tuple-element.36), channel_id=1, source_target_pairs={{0,8},{4,12},{8,0},{12,4},{1,9},{5,13},{9,1},{13,5},{2,10},{6,14},... | collective-permute-start | bytes 884744 | tf_op jit(solution)/shard_map/ppermute | solution.py:414
  40.5 10.1 %collective-permute-start.1 = (bf16[2,144,512]{2,1,0:T(8,128)(2,1)S(1)}, bf16[2,144,512]{2,1,0:T(8,128)(2,1)S(1)}, u32[]{:S(2)}, u32[]{:S(2)}) collective-permute-start(bf16[2,144,512]{2,1,0:T(8,128)(2,1)S(1)} %get-tuple-element.36), channel_id=1, source_target_pairs={{0,4},{4,8},{8,12},{12,0},{1,5},{5,9},{9,13},{13,1},{2,6},{6,10},{... | collective-permute-start | bytes 884744 | tf_op jit(solution)/shard_map/ppermute | solution.py:414
  43.0 8.8 %collective-permute-start.3 = (bf16[2,144,512]{2,1,0:T(8,128)(2,1)S(1)}, bf16[2,144,512]{2,1,0:T(8,128)(2,1)S(1)}, u32[]{:S(2)}, u32[]{:S(2)}) collective-permute-start(bf16[2,144,512]{2,1,0:T(8,128)(2,1)S(1)} %get-tuple-element.36), channel_id=1, source_target_pairs={{0,12},{4,0},{8,4},{12,8},{1,13},{5,1},{9,5},{13,9},{2,14},{6,2},{... | collective-permute-start | bytes 884744 | tf_op jit(solution)/shard_map/ppermute | solution.py:414
  52.0 2.0 %copy-start = (bf16[2,4,144,512]{3,2,1,0:T(8,128)(2,1)}, bf16[2,4,144,512]{3,2,1,0:T(8,128)(2,1)S(1)}, u32[]{:S(2)}) copy-start(bf16[2,4,144,512]{3,2,1,0:T(8,128)(2,1)S(1)} %pad_maximum_fusion.keys_hbm) | copy-start | bytes 3538948
  52.0 9.1 %collective-permute-start.4 = (bf16[2,4,144,512]{3,2,1,0:T(8,128)(2,1)S(1)}, bf16[2,4,144,512]{3,2,1,0:T(8,128)(2,1)S(1)}, u32[]{:S(2)}, u32[]{:S(2)}) collective-permute-start(bf16[2,4,144,512]{3,2,1,0:T(8,128)(2,1)S(1)} %pad_maximum_fusion.keys_hbm), channel_id=1, source_target_pairs={{0,1},{1,0},{2,3},{3,2},{4,5},{5,4},{6,7},{7,6},{8,9},{9,8},{10,11... | collective-permute-start | bytes 3538952 | tf_op jit(solution)/shard_map/ppermute | solution.py:435
  53.9 0.8 copy-start.1
  61.1 1.0 copy-start.5
  72.6 6.5 %copy-start.6 = (bf16[4,672,128]{2,1,0:T(8,128)(2,1)S(1)}, bf16[4,672,128]{2,1,0:T(8,128)(2,1)}, u32[]{:S(2)}) copy-start(bf16[4,672,128]{2,1,0:T(8,128)(2,1)} %get-tuple-element.31) | copy-start | bytes 2064388
  72.6 4.4 %collective-permute-start.5 = (bf16[4,576,128]{2,1,0:T(8,128)(2,1)}, bf16[4,576,128]{2,1,0:T(8,128)(2,1)S(1)}, u32[]{:S(2)}, u32[]{:S(2)}) collective-permute-start(bf16[4,576,128]{2,1,0:T(8,128)(2,1)} %get-tuple-element.29), channel_id=1, source_target_pairs={{0,1},{1,0},{2,3},{3,2},{4,5},{5,4},{6,7},{7,6},{8,9},{9,8},{10,11... | collective-permute-start | bytes 1769480 | tf_op jit(solution)/shard_map/ppermute | solution.py:466
  79.0 8.1 %collective-permute-start.6 = (bf16[4,672,128]{2,1,0:T(8,128)(2,1)S(1)}, bf16[4,672,128]{2,1,0:T(8,128)(2,1)S(1)}, u32[]{:S(2)}, u32[]{:S(2)}) collective-permute-start(bf16[4,672,128]{2,1,0:T(8,128)(2,1)S(1)} %copy-done.6), channel_id=1, source_target_pairs={{0,1},{1,0},{2,3},{3,2},{4,5},{5,4},{6,7},{7,6},{8,9},{9,8},{10,11... | collective-permute-start | bytes 2064392 | tf_op jit(solution)/shard_map/ppermute | solution.py:469
  81.3 19.3 %all-to-all-start.2 = ((bf16[4,576,128]{2,1,0:T(8,128)(2,1)}), bf16[4,576,128]{2,1,0:T(8,128)(2,1)S(1)}, u32[]{:S(2)}, u32[]{:S(2)}) async-start(bf16[4,576,128]{2,1,0:T(8,128)(2,1)} %add_convert_fusion), calls=%async_computation.2 | async-start | bytes 1179648 | tf_op jit(solution)/shard_map/all_to_all | solution.py:473
  87.1 23.2 %copy-start.4 = (bf16[4,672,128]{2,1,0:T(8,128)(2,1)}, bf16[4,672,128]{2,1,0:T(8,128)(2,1)S(1)}, u32[]{:S(2)}) copy-start(bf16[4,672,128]{2,1,0:T(8,128)(2,1)S(1)} %collective-permute-done.6.got_ref) | copy-start | bytes 2064388
  87.1 23.2 %collective-permute-start.7 = (bf16[4,2,48,128]{3,2,1,0:T(8,128)(2,1)S(1)}, bf16[4,2,48,128]{3,2,1,0:T(8,128)(2,1)S(1)}, u32[]{:S(2)}, u32[]{:S(2)}) collective-permute-start(bf16[4,2,48,128]{3,2,1,0:T(8,128)(2,1)S(1)} %pad_maximum_fusion.3), channel_id=1, source_target_pairs={{0,2},{2,0},{1,3},{3,1},{4,6},{6,4},{5,7},{7,5},{8,10},{10,8},{9,1... | collective-permute-start | bytes 294920 | tf_op jit(solution)/shard_map/ppermute | solution.py:472
  100.7 22.5 %collective-permute-start.8 = (bf16[576,128]{1,0:T(8,128)(2,1)S(1)}, bf16[576,128]{1,0:T(8,128)(2,1)S(1)}, u32[]{:S(2)}, u32[]{:S(2)}) collective-permute-start(bf16[576,128]{1,0:T(8,128)(2,1)S(1)} %reduce_sum.22), channel_id=1, source_target_pairs={{0,2},{2,0},{1,3},{3,1},{4,6},{6,4},{5,7},{7,5},{8,10},{10,8},{9,1... | collective-permute-start | bytes 442376 | tf_op jit(solution)/shard_map/ppermute | solution.py:475
  110.3 0.6 copy-start.8
  113.3 14.9 %all-to-all-start.1 = ((bf16[4,768,128]{2,1,0:T(8,128)(2,1)}), bf16[4,768,128]{2,1,0:T(8,128)(2,1)S(1)}, u32[]{:S(2)}, u32[]{:S(2)}) async-start(bf16[4,768,128]{2,1,0:T(8,128)(2,1)} %shard_map.114), calls=%async_computation.1 | async-start | bytes 1572864 | tf_op jit(solution)/shard_map/all_to_all | solution.py:477
  123.2 0.7 copy-start.7
  125.4 2.9 %copy-start.3 = (bf16[64,128]{1,0:T(8,128)(2,1)S(1)}, bf16[64,128]{1,0:T(8,128)(2,1)}, u32[]{:S(2)}) copy-start(bf16[64,128]{1,0:T(8,128)(2,1)} %get-tuple-element.34) | copy-start | bytes 49156
  125.4 3.5 %copy-start.2 = (bf16[128,512]{1,0:T(8,128)(2,1)S(1)}, bf16[128,512]{1,0:T(8,128)(2,1)}, u32[]{:S(2)}) copy-start(bf16[128,512]{1,0:T(8,128)(2,1)} %get-tuple-element.33) | copy-start | bytes 393220

commit v4 on v3

--- a/solution.py
+++ b/solution.py
@@ -21,6 +21,7 @@
 LOWEST = -1e29
 HIDDEN = -1e30
 EXPONENT = math.log2(math.e) * WIDTH ** (-0.5)
+FIRST_FLOPS = 5_000_000_000
 ORDER_FLOPS = 20_000_000_000
 NEAR_FLOPS = 6_000_000_000
 
@@ -46,14 +47,27 @@
         keyed[span, LATENT:] = jnp.transpose(rot)
 
 
-def forward_chunk(n, base, carry, bound_ref, rel, keyed, q_cat, o_lat, expo, dprob):
+def owner(y, z, c):
+    return (y * N_Z + z) * N_C + c
+
+
+def behind(y, j):
+    return lax.rem(y - j + N_Y, N_Y)
+
+
+def forward_chunk(n, other, base, carry, where_ref, rel, keyed, q_cat, o_lat, expo, dprob):
     top, total, delta = carry
     block = rel.shape[0]
     span = slice(base, base + N_Y * block)
     scores = dot(keyed[span, :], q_cat[...], 1, 1)
     dp = dot(keyed[span, :LATENT], o_lat[...], 1, 1)
     dprob[span, :] = dp
-    visible = [rel[...] <= bound_ref[n * N_Y + j] for j in range(N_Y)]
+    y, z, c, offset = (where_ref[i] for i in range(4))
+    z_of = z if n == 1 else 1 - z
+    c_of = 1 - c if other else c
+    visible = [
+        rel[...] <= offset - owner(behind(y, j), z_of, c_of) * block for j in range(N_Y)
+    ]
     parts = [
         jnp.where(visible[j], scores[j * block : (j + 1) * block], HIDDEN)
         for j in range(N_Y)
@@ -79,7 +93,7 @@
 
 
 def first_kernel(
-    bound_ref,
+    where_ref,
     qg_hbm,
     wk_hbm,
     wv_hbm,
@@ -140,7 +154,7 @@
     for n in range(N_Z):
         unpack_keys(packed.at[n], keyed, n * chunk)
         carry = forward_chunk(
-            n, n * chunk, carry, bound_ref, rel, keyed, q_cat, o_lat, expo, dprob
+            n, False, n * chunk, carry, where_ref, rel, keyed, q_cat, o_lat, expo, dprob
         )
         span = pl.ds(n * chunk, chunk)
         for i, (mine, out) in enumerate(
@@ -159,9 +173,7 @@
 
 
 def second_kernel(
-    bound_ref,
-    row_ref,
-    slot_ref,
+    where_ref,
     stats_ref,
     q_cat_hbm,
     o_lat_hbm,
@@ -189,6 +201,7 @@
     out_sem,
 ):
     scale = WIDTH ** (-0.5)
+    y, z, c = (where_ref[i] for i in range(3))
     heads = wk_ref.shape[1] // NOPE
     stacked = q_cat.shape[0]
     count = stacked // heads
@@ -221,7 +234,7 @@
     for n in range(N_Z):
         unpack_keys(packed.at[n], keyed, n * chunk)
         carry = forward_chunk(
-            n, n * chunk, carry, bound_ref, rel, keyed, q_cat, o_lat, expo, dprob
+            n, True, n * chunk, carry, where_ref, rel, keyed, q_cat, o_lat, expo, dprob
         )
         tops.append(carry[0])
     tops += [stats_ref[n : n + 1, :] for n in range(N_Z)]
@@ -243,7 +256,7 @@
         d_rot = d_key[:, LATENT:].astype(BF16)
         for j in range(N_Y):
             rows = slice(j * block, (j + 1) * block)
-            place = (d_far, d_near)[z_slot].at[c_slot, slot_ref[j]]
+            place = (d_far, d_near)[z_slot].at[c_slot, behind(y, j)]
             for a in range(folds):
                 place[a * block : (a + 1) * block, :] = d_lat[
                     rows, a * LANES : (a + 1) * LANES
@@ -271,7 +284,9 @@
         for j in range(N_Y):
             pieces = []
             for dz in range(N_Z):
-                start = pl.multiple_of(row_ref[(n * N_Y + j) * N_Z + dz], few)
+                z_of = z if dz == 1 else 1 - z
+                c_of = c if n == 1 else 1 - c
+                start = pl.multiple_of(owner(j, z_of, c_of) * few, few)
                 for a in range(heads * WIDTH // LANES):
                     pieces.append(dq_ref[pl.ds(start, few), a * LANES : (a + 1) * LANES])
             d_near[n, j, slab:, :] = jnp.concatenate(pieces, axis=0).astype(BF16)
@@ -284,7 +299,7 @@
         store.wait()
 
 
-def attention(bounds_mine, bounds_other, starts, slots, qg, w_key, w_value, mine, other):
+def attention(where, qg, w_key, w_value, mine, other):
     count = qg.shape[0]
     heads = w_key.shape[1] // NOPE
     stacked = heads * count
@@ -326,14 +341,14 @@
         ],
         compiler_params=pltpu.CompilerParams(vmem_limit_bytes=56 * 2**20),
         cost_estimate=pl.CostEstimate(
-            flops=ORDER_FLOPS, bytes_accessed=12 * half * stacked, transcendentals=half * stacked
+            flops=FIRST_FLOPS, bytes_accessed=12 * half * stacked, transcendentals=half * stacked
         ),
-    )(bounds_mine, qg, w_key, w_value, mine)
+    )(where, qg, w_key, w_value, mine)
     return pl.pallas_call(
         second_kernel,
         out_shape=[jax.ShapeDtypeStruct((N_Y, slab, LANES), BF16)] * N_C
         + [jax.ShapeDtypeStruct((N_Y, near_slab, LANES), BF16)] * N_C,
-        in_specs=[smem] * 3 + [vmem] + [hbm] * 7,
+        in_specs=[smem, vmem] + [hbm] * 7,
         out_specs=[hbm] * 4,
         scratch_shapes=[
             pltpu.VMEM(w_key.shape, BF16),
@@ -356,7 +371,7 @@
             bytes_accessed=16 * half * stacked,
             transcendentals=half * stacked,
         ),
-    )(bounds_other, starts, slots, stats, q_cat, o_lat, w_key, other, keyed, expo, dprob)
+    )(where, stats, q_cat, o_lat, w_key, other, keyed, expo, dprob)
 
 
 def payload_kernel(mine_ref, got_ref, dq_ref, out_ref):
@@ -434,28 +449,9 @@
     mine = jnp.stack([both] + [shift(both, s) for s in range(1, N_Y)], axis=1)
     other = lax.ppermute(mine, "c", SWAP)
 
-    steps = jnp.arange(N_Y, dtype=jnp.int32)
-
-    def owner(y_of, z_of, c_of):
-        return ((y_of * N_Z + z_of) * N_C + c_of).astype(jnp.int32)
-
-    shifted = lax.rem(y - steps + N_Y, N_Y)
-    owners = [
-        jnp.concatenate([owner(shifted, z ^ dz, c_of) for dz in (1, 0)])
-        for c_of in (c, c ^ 1)
-    ]
-    bounds_mine, bounds_other = (offset[0] - of * block for of in owners)
-    starts = jnp.stack(
-        [
-            owner(steps[:, None], z ^ jnp.array([[1, 0]]), c ^ dc).reshape(-1)
-            for dc in (1, 0)
-        ]
-    ).reshape(-1)
+    where = jnp.stack([y, z, c, offset[0]]).astype(jnp.int32)
     d_other, d_mine, d_near_other, d_near_mine = attention(
-        bounds_mine,
-        bounds_other,
-        starts * few,
-        shifted.astype(jnp.int32),
+        where,
         qg,
         w_key,
         w_value,

time: 131 us -> 133 us (1.015)
  the two profiles are of different devices: /device:TPU:38 before, /device:TPU:32 now
where the time goes in v4:
time: 133 us; the launch traced here: 132 us
  starting transfers between devices  69.6 us (52%)
  waiting for transfers between devices  27.3 us (21%)
  Pallas kernels  21.1 us (16%)
  other arithmetic  6.91 us (5%)
  local copies, waits for them, and re-layouts  5.6 us (4%)
  between operations  1.54 us (1%)
    ppermute x1, starting transfers between devices, on_device(): far = lax.ppermute(pack, 'z', SWAP)  14.8 us
    ppermute x1, starting transfers between devices, on_device(): lax.ppermute(jnp.stack([p[:, :piece] for p in pieces], axis=1), 'z', SWAP)  13.4 us
    ppermute x1, waiting for transfers between devices, on_device(): far = lax.ppermute(pack, 'z', SWAP)  12.1 us
    ppermute x3, starting transfers between devices, shift(): return lax.ppermute(block, 'y', [(i, (i + by) % N_Y) for i in range(N_Y)])  11.9 us
    pallas_call x1, Pallas kernels, attention(): pl.pallas_call(second_kernel, out_shape=[jax.ShapeDtypeStruct((N_Y, slab,...  10.4 us
    ppermute x1, starting transfers between devices, on_device(): back = lax.ppermute(leaving, 'z', SWAP)  9.61 us
    ppermute x1, waiting for transfers between devices, on_device(): back = lax.ppermute(leaving, 'z', SWAP)  7.29 us
    pallas_call x1, Pallas kernels, attention(): pl.pallas_call(first_kernel, out_shape=middle, in_specs=[smem] + [hbm] *...  6.75 us
  transfers between devices with their start and end apart: 12, of which 6 were waited for; matrix products, arithmetic and copies ran while one was open for 3% of the time, Pallas kernels for 8%

profile of v4, /device:TPU:32, one launch (start us, length us, event | category | flops | bytes accessed | tf_op | source)
XLA Modules:
  0.0 132.0 jit_solution(6732215432384920391)
XLA Ops:
  0.6 0.7 copy.10
  1.4 0.9 constant_dynamic-update-slice_fusion
  2.3 14.8 %collective-permute-start = (bf16[144,512]{1,0:T(8,128)(2,1)S(1)}, bf16[144,512]{1,0:T(8,128)(2,1)S(1)}, u32[]{:S(2)}, u32[]{:S(2)}) collective-permute-start(bf16[144,512]{1,0:T(8,128)(2,1)S(1)} %bitcast_dynamic-update-slice_fusion), channel_id=1, source_target_pairs={{0,2},{2,0},{1,3},{3,1},{4,6},{6,4},{5,7},{7,5},{8,10},{10,8},{9,1... | collective-permute-start | bytes 442376 | tf_op jit(solution)/shard_map/ppermute | solution.py:442
  17.1 1.7 %pad_maximum_fusion.1 = bf16[8,16,1280]{2,0,1:T(8,128)(2,1)} fusion(bf16[8,16,512]{2,0,1:T(8,128)(2,1)} %bitcast.58, bf16[8,16,768]{2,0,1:T(8,128)(2,1)} %bitcast.56), kind=kLoop, calls=%fused_computation.3 | loop fusion | flops 655360 | bytes 655360 | tf_op jit(solution)/shard_map/concatenate | solution.py:443
  18.9 4.6 %all-to-all-start = ((bf16[8,16,1280]{2,0,1:T(8,128)(2,1)}), bf16[8,16,1280]{2,0,1:T(8,128)(2,1)S(1)}, u32[]{:S(2)}, u32[]{:S(2)}) async-start(bf16[8,16,1280]{2,0,1:T(8,128)(2,1)} %bitcast.9), calls=%async_computation | async-start | bytes 655360 | tf_op jit(solution)/shard_map/all_to_all | solution.py:447
  23.4 12.1 %collective-permute-done = bf16[144,512]{1,0:T(8,128)(2,1)S(1)} collective-permute-done((bf16[144,512]{1,0:T(8,128)(2,1)S(1)}, bf16[144,512]{1,0:T(8,128)(2,1)S(1)}, u32[]{:S(2)}, u32[]{:S(2)}) %collective-permute-start) | collective-permute-done | bytes 147488 | tf_op jit(solution)/shard_map/ppermute | solution.py:442
  35.6 4.9 %collective-permute-start.2 = (bf16[2,144,512]{2,1,0:T(8,128)(2,1)S(1)}, bf16[2,144,512]{2,1,0:T(8,128)(2,1)S(1)}, u32[]{:S(2)}, u32[]{:S(2)}) collective-permute-start(bf16[2,144,512]{2,1,0:T(8,128)(2,1)S(1)} %get-tuple-element.36), channel_id=1, source_target_pairs={{0,8},{4,12},{8,0},{12,4},{1,9},{5,13},{9,1},{13,5},{2,10},{6,14},... | collective-permute-start | bytes 884744 | tf_op jit(solution)/shard_map/ppermute | solution.py:429
  40.5 2.5 %collective-permute-start.1 = (bf16[2,144,512]{2,1,0:T(8,128)(2,1)S(1)}, bf16[2,144,512]{2,1,0:T(8,128)(2,1)S(1)}, u32[]{:S(2)}, u32[]{:S(2)}) collective-permute-start(bf16[2,144,512]{2,1,0:T(8,128)(2,1)S(1)} %get-tuple-element.36), channel_id=1, source_target_pairs={{0,4},{4,8},{8,12},{12,0},{1,5},{5,9},{9,13},{13,1},{2,6},{6,10},{... | collective-permute-start | bytes 884744 | tf_op jit(solution)/shard_map/ppermute | solution.py:429
  43.0 4.6 %collective-permute-start.3 = (bf16[2,144,512]{2,1,0:T(8,128)(2,1)S(1)}, bf16[2,144,512]{2,1,0:T(8,128)(2,1)S(1)}, u32[]{:S(2)}, u32[]{:S(2)}) collective-permute-start(bf16[2,144,512]{2,1,0:T(8,128)(2,1)S(1)} %get-tuple-element.36), channel_id=1, source_target_pairs={{0,12},{4,0},{8,4},{12,8},{1,13},{5,1},{9,5},{13,9},{2,14},{6,2},{... | collective-permute-start | bytes 884744 | tf_op jit(solution)/shard_map/ppermute | solution.py:429
  47.6 0.0 collective-permute-done.2
  47.6 3.0 %collective-permute-done.1 = bf16[2,144,512]{2,1,0:T(8,128)(2,1)S(1)} collective-permute-done((bf16[2,144,512]{2,1,0:T(8,128)(2,1)S(1)}, bf16[2,144,512]{2,1,0:T(8,128)(2,1)S(1)}, u32[]{:S(2)}, u32[]{:S(2)}) %collective-permute-start.1) | collective-permute-done | bytes 294944 | tf_op jit(solution)/shard_map/ppermute | solution.py:429
  50.6 1.2 collective-permute-done.3
  51.8 0.1 pad_maximum_fusion.keys_hbm
  52.0 1.9 %collective-permute-start.4 = (bf16[2,4,144,512]{3,2,1,0:T(8,128)(2,1)S(1)}, bf16[2,4,144,512]{3,2,1,0:T(8,128)(2,1)S(1)}, u32[]{:S(2)}, u32[]{:S(2)}) collective-permute-start(bf16[2,4,144,512]{3,2,1,0:T(8,128)(2,1)S(1)} %pad_maximum_fusion.keys_hbm), channel_id=1, source_target_pairs={{0,1},{1,0},{2,3},{3,2},{4,5},{5,4},{6,7},{7,6},{8,9},{9,8},{10,11... | collective-permute-start | bytes 3538952 | tf_op jit(solution)/shard_map/ppermute | solution.py:450
  54.5 0.6 pad_add_fusion.where_ref
  55.2 0.0 all-to-all-done
  55.2 0.0 copy-done
  55.2 0.8 copy-done.1
  56.0 6.8 %shard_map.94 = (bf16[512,576]{1,0:T(8,128)(2,1)}, bf16[512,512]{1,0:T(8,128)(2,1)}, bf16[1024,576]{1,0:T(8,128)(2,1)}, f32[1024,512]{1,0:T(8,128)}, f32[1024,512]{1,0:T(8,128)}, /*index=5*/f32[8,512]{1,0:T(8,128)}) custom-call(s32[4]{0:T(128)} %pad_add_fusion.where_ref, bf16[128,1280]{1,0:T(8,128)(2,1)} %bitcast.51, bf16[512,512]{1,0:T(8,128)(2,1)} %wk_hbm.3, ...), custom_call_target="tpu_custom_call" | custom-call | flops 5000000000 | bytes 6291456 | tf_op jit(solution)/shard_map/pallas_call | solution.py:323
  62.7 0.0 collective-permute-done.4.keys_hbm
  62.8 1.0 copy-done.5
  63.8 10.4 %shard_map.95 = (bf16[4,576,128]{2,1,0:T(8,128)(2,1)}, bf16[4,576,128]{2,1,0:T(8,128)(2,1)}, bf16[4,672,128]{2,1,0:T(8,128)(2,1)}, bf16[4,672,128]{2,1,0:T(8,128)(2,1)}) custom-call(s32[4]{0:T(128)} %pad_add_fusion.where_ref, f32[8,512]{1,0:T(8,128)} %get-tuple-element.21.stats_ref, bf16[512,576]{1,0:T(8,128)(2,1)} %get-tuple-element.22.q_cat_hbm, ...), custom_call_target="tpu_custom_call" | custom-call | flops 4630511616 | bytes 8388608 | tf_op jit(solution)/shard_map/pallas_call | solution.py:347
  74.2 2.5 %collective-permute-start.5 = (bf16[4,576,128]{2,1,0:T(8,128)(2,1)}, bf16[4,576,128]{2,1,0:T(8,128)(2,1)S(1)}, u32[]{:S(2)}, u32[]{:S(2)}) collective-permute-start(bf16[4,576,128]{2,1,0:T(8,128)(2,1)} %get-tuple-element.29), channel_id=1, source_target_pairs={{0,1},{1,0},{2,3},{3,2},{4,5},{5,4},{6,7},{7,6},{8,9},{9,8},{10,11... | collective-permute-start | bytes 1769480 | tf_op jit(solution)/shard_map/ppermute | solution.py:462
  76.7 1.8 %collective-permute-done.5 = bf16[4,576,128]{2,1,0:T(8,128)(2,1)S(1)} collective-permute-done((bf16[4,576,128]{2,1,0:T(8,128)(2,1)}, bf16[4,576,128]{2,1,0:T(8,128)(2,1)S(1)}, u32[]{:S(2)}, u32[]{:S(2)}) %collective-permute-start.5) | collective-permute-done | bytes 589856 | tf_op jit(solution)/shard_map/ppermute | solution.py:462
  78.5 2.1 %add_convert_fusion = bf16[4,576,128]{2,1,0:T(8,128)(2,1)} fusion(bf16[4,576,128]{2,1,0:T(8,128)(2,1)S(1)} %collective-permute-done.5, bf16[4,576,128]{2,1,0:T(8,128)(2,1)} %get-tuple-element.28), kind=kLoop, calls=%fused_computation.2 | loop fusion | flops 1179648 | bytes 1769472 | tf_op jit(solution)/shard_map/convert_element_type | solution.py:463
  80.6 2.3 %collective-permute-start.6 = (bf16[4,672,128]{2,1,0:T(8,128)(2,1)S(1)}, bf16[4,672,128]{2,1,0:T(8,128)(2,1)S(1)}, u32[]{:S(2)}, u32[]{:S(2)}) collective-permute-start(bf16[4,672,128]{2,1,0:T(8,128)(2,1)S(1)} %copy-done.6), channel_id=1, source_target_pairs={{0,1},{1,0},{2,3},{3,2},{4,5},{5,4},{6,7},{7,6},{8,9},{9,8},{10,11... | collective-permute-start | bytes 2064392 | tf_op jit(solution)/shard_map/ppermute | solution.py:465
  82.9 5.0 %all-to-all-start.2 = ((bf16[4,576,128]{2,1,0:T(8,128)(2,1)}), bf16[4,576,128]{2,1,0:T(8,128)(2,1)S(1)}, u32[]{:S(2)}, u32[]{:S(2)}) async-start(bf16[4,576,128]{2,1,0:T(8,128)(2,1)} %add_convert_fusion), calls=%async_computation.2 | async-start | bytes 1179648 | tf_op jit(solution)/shard_map/all_to_all | solution.py:469
  87.9 0.8 slice_bitcast_fusion.1
  88.7 0.0 collective-permute-done.6.got_ref
  88.7 13.4 %collective-permute-start.7 = (bf16[4,2,48,128]{3,2,1,0:T(8,128)(2,1)S(1)}, bf16[4,2,48,128]{3,2,1,0:T(8,128)(2,1)S(1)}, u32[]{:S(2)}, u32[]{:S(2)}) collective-permute-start(bf16[4,2,48,128]{3,2,1,0:T(8,128)(2,1)S(1)} %pad_maximum_fusion.3), channel_id=1, source_target_pairs={{0,2},{2,0},{1,3},{3,1},{4,6},{6,4},{5,7},{7,5},{8,10},{10,8},{9,1... | collective-permute-start | bytes 294920 | tf_op jit(solution)/shard_map/ppermute | solution.py:468
  102.2 0.0 all-to-all-done.2
  102.2 0.1 reduce_sum.22
  102.3 9.6 %collective-permute-start.8 = (bf16[576,128]{1,0:T(8,128)(2,1)S(1)}, bf16[576,128]{1,0:T(8,128)(2,1)S(1)}, u32[]{:S(2)}, u32[]{:S(2)}) collective-permute-start(bf16[576,128]{1,0:T(8,128)(2,1)S(1)} %reduce_sum.22), channel_id=1, source_target_pairs={{0,2},{2,0},{1,3},{3,1},{4,6},{6,4},{5,7},{7,5},{8,10},{10,8},{9,1... | collective-permute-start | bytes 442376 | tf_op jit(solution)/shard_map/ppermute | solution.py:471
  111.9 0.0 collective-permute-done.7.dq_ref
  111.9 0.0 copy-start.8
  111.9 0.6 copy-done.8
  112.6 2.3 %shard_map.96 = bf16[4,768,128]{2,1,0:T(8,128)(2,1)} custom-call(bf16[4,672,128]{2,1,0:T(8,128)(2,1)} %get-tuple-element.27.mine_ref, bf16[4,672,128]{2,1,0:T(8,128)(2,1)} %copy-done.4, bf16[4,2,48,128]{3,2,1,0:T(8,128)(2,1)} %copy-done.8), custom_call_target="tpu_custom_call" | custom-call | flops 6000000000 | bytes 2064384 | tf_op jit(solution)/shard_map/pallas_call | solution.py:393
  114.9 3.5 %all-to-all-start.1 = ((bf16[4,768,128]{2,1,0:T(8,128)(2,1)}), bf16[4,768,128]{2,1,0:T(8,128)(2,1)S(1)}, u32[]{:S(2)}, u32[]{:S(2)}) async-start(bf16[4,768,128]{2,1,0:T(8,128)(2,1)} %shard_map.96), calls=%async_computation.1 | async-start | bytes 1572864 | tf_op jit(solution)/shard_map/all_to_all | solution.py:473
  118.4 7.3 %collective-permute-done.8.packed_ref = bf16[576,128]{1,0:T(8,128)(2,1)S(1)} collective-permute-done((bf16[576,128]{1,0:T(8,128)(2,1)S(1)}, bf16[576,128]{1,0:T(8,128)(2,1)S(1)}, u32[]{:S(2)}, u32[]{:S(2)}) %collective-permute-start.8) | collective-permute-done | bytes 147488 | tf_op jit(solution)/shard_map/ppermute | solution.py:471
  125.7 0.7 copy-done.7
  126.4 1.6 %shard_map.97 = (bf16[128,512]{1,0:T(8,128)(2,1)}, bf16[64,128]{1,0:T(8,128)(2,1)}) custom-call(bf16[576,128]{1,0:T(8,128)(2,1)} %copy-done.7), custom_call_target="tpu_custom_call" | custom-call | flops 20000000000 | bytes 294912 | tf_op jit(solution)/shard_map/pallas_call | solution.py:414
  128.0 1.9 %all-to-all-done.1 = bf16[4,768,128]{2,1,0:T(8,128)(2,1)S(1)} async-done(((bf16[4,768,128]{2,1,0:T(8,128)(2,1)}), bf16[4,768,128]{2,1,0:T(8,128)(2,1)S(1)}, u32[]{:S(2)}, u32[]{:S(2)}) %all-to-all-start.1) | async-done | bytes 786464 | tf_op jit(solution)/shard_map/all_to_all | solution.py:473
  129.8 0.1 convert_reduce_fusion
  129.9 0.0 copy-done.3
  129.9 0.6 fusion.2
  130.5 0.0 copy-done.2
  130.5 0.7 fusion
  131.3 0.7 reverse_select_fusion
  (17 shorter events, 0.2 us)
Async XLA Ops:
  2.3 33.3 %collective-permute-start = (bf16[144,512]{1,0:T(8,128)(2,1)S(1)}, bf16[144,512]{1,0:T(8,128)(2,1)S(1)}, u32[]{:S(2)}, u32[]{:S(2)}) collective-permute-start(bf16[144,512]{1,0:T(8,128)(2,1)S(1)} %bitcast_dynamic-update-slice_fusion), channel_id=1, source_target_pairs={{0,2},{2,0},{1,3},{3,1},{4,6},{6,4},{5,7},{7,5},{8,10},{10,8},{9,1... | collective-permute-start | bytes 442376 | tf_op jit(solution)/shard_map/ppermute | solution.py:442
  18.9 36.3 %all-to-all-start = ((bf16[8,16,1280]{2,0,1:T(8,128)(2,1)}), bf16[8,16,1280]{2,0,1:T(8,128)(2,1)S(1)}, u32[]{:S(2)}, u32[]{:S(2)}) async-start(bf16[8,16,1280]{2,0,1:T(8,128)(2,1)} %bitcast.9), calls=%async_computation | async-start | bytes 655360 | tf_op jit(solution)/shard_map/all_to_all | solution.py:447
  35.6 12.0 %collective-permute-start.2 = (bf16[2,144,512]{2,1,0:T(8,128)(2,1)S(1)}, bf16[2,144,512]{2,1,0:T(8,128)(2,1)S(1)}, u32[]{:S(2)}, u32[]{:S(2)}) collective-permute-start(bf16[2,144,512]{2,1,0:T(8,128)(2,1)S(1)} %get-tuple-element.36), channel_id=1, source_target_pairs={{0,8},{4,12},{8,0},{12,4},{1,9},{5,13},{9,1},{13,5},{2,10},{6,14},... | collective-permute-start | bytes 884744 | tf_op jit(solution)/shard_map/ppermute | solution.py:429
  40.5 10.1 %collective-permute-start.1 = (bf16[2,144,512]{2,1,0:T(8,128)(2,1)S(1)}, bf16[2,144,512]{2,1,0:T(8,128)(2,1)S(1)}, u32[]{:S(2)}, u32[]{:S(2)}) collective-permute-start(bf16[2,144,512]{2,1,0:T(8,128)(2,1)S(1)} %get-tuple-element.36), channel_id=1, source_target_pairs={{0,4},{4,8},{8,12},{12,0},{1,5},{5,9},{9,13},{13,1},{2,6},{6,10},{... | collective-permute-start | bytes 884744 | tf_op jit(solution)/shard_map/ppermute | solution.py:429
  43.0 8.8 %collective-permute-start.3 = (bf16[2,144,512]{2,1,0:T(8,128)(2,1)S(1)}, bf16[2,144,512]{2,1,0:T(8,128)(2,1)S(1)}, u32[]{:S(2)}, u32[]{:S(2)}) collective-permute-start(bf16[2,144,512]{2,1,0:T(8,128)(2,1)S(1)} %get-tuple-element.36), channel_id=1, source_target_pairs={{0,12},{4,0},{8,4},{12,8},{1,13},{5,1},{9,5},{13,9},{2,14},{6,2},{... | collective-permute-start | bytes 884744 | tf_op jit(solution)/shard_map/ppermute | solution.py:429
  52.0 3.2 %copy-start = (bf16[2,4,144,512]{3,2,1,0:T(8,128)(2,1)}, bf16[2,4,144,512]{3,2,1,0:T(8,128)(2,1)S(1)}, u32[]{:S(2)}) copy-start(bf16[2,4,144,512]{3,2,1,0:T(8,128)(2,1)S(1)} %pad_maximum_fusion.keys_hbm) | copy-start | bytes 3538948
  52.0 10.8 %collective-permute-start.4 = (bf16[2,4,144,512]{3,2,1,0:T(8,128)(2,1)S(1)}, bf16[2,4,144,512]{3,2,1,0:T(8,128)(2,1)S(1)}, u32[]{:S(2)}, u32[]{:S(2)}) collective-permute-start(bf16[2,4,144,512]{3,2,1,0:T(8,128)(2,1)S(1)} %pad_maximum_fusion.keys_hbm), channel_id=1, source_target_pairs={{0,1},{1,0},{2,3},{3,2},{4,5},{5,4},{6,7},{7,6},{8,9},{9,8},{10,11... | collective-permute-start | bytes 3538952 | tf_op jit(solution)/shard_map/ppermute | solution.py:450
  55.2 0.8 copy-start.1
  62.7 1.0 copy-start.5
  74.2 6.5 %copy-start.6 = (bf16[4,672,128]{2,1,0:T(8,128)(2,1)S(1)}, bf16[4,672,128]{2,1,0:T(8,128)(2,1)}, u32[]{:S(2)}) copy-start(bf16[4,672,128]{2,1,0:T(8,128)(2,1)} %get-tuple-element.31) | copy-start | bytes 2064388
  74.2 4.4 %collective-permute-start.5 = (bf16[4,576,128]{2,1,0:T(8,128)(2,1)}, bf16[4,576,128]{2,1,0:T(8,128)(2,1)S(1)}, u32[]{:S(2)}, u32[]{:S(2)}) collective-permute-start(bf16[4,576,128]{2,1,0:T(8,128)(2,1)} %get-tuple-element.29), channel_id=1, source_target_pairs={{0,1},{1,0},{2,3},{3,2},{4,5},{5,4},{6,7},{7,6},{8,9},{9,8},{10,11... | collective-permute-start | bytes 1769480 | tf_op jit(solution)/shard_map/ppermute | solution.py:462
  80.6 8.0 %collective-permute-start.6 = (bf16[4,672,128]{2,1,0:T(8,128)(2,1)S(1)}, bf16[4,672,128]{2,1,0:T(8,128)(2,1)S(1)}, u32[]{:S(2)}, u32[]{:S(2)}) collective-permute-start(bf16[4,672,128]{2,1,0:T(8,128)(2,1)S(1)} %copy-done.6), channel_id=1, source_target_pairs={{0,1},{1,0},{2,3},{3,2},{4,5},{5,4},{6,7},{7,6},{8,9},{9,8},{10,11... | collective-permute-start | bytes 2064392 | tf_op jit(solution)/shard_map/ppermute | solution.py:465
  82.9 19.3 %all-to-all-start.2 = ((bf16[4,576,128]{2,1,0:T(8,128)(2,1)}), bf16[4,576,128]{2,1,0:T(8,128)(2,1)S(1)}, u32[]{:S(2)}, u32[]{:S(2)}) async-start(bf16[4,576,128]{2,1,0:T(8,128)(2,1)} %add_convert_fusion), calls=%async_computation.2 | async-start | bytes 1179648 | tf_op jit(solution)/shard_map/all_to_all | solution.py:469
  88.7 23.2 %copy-start.4 = (bf16[4,672,128]{2,1,0:T(8,128)(2,1)}, bf16[4,672,128]{2,1,0:T(8,128)(2,1)S(1)}, u32[]{:S(2)}) copy-start(bf16[4,672,128]{2,1,0:T(8,128)(2,1)S(1)} %collective-permute-done.6.got_ref) | copy-start | bytes 2064388
  88.7 23.2 %collective-permute-start.7 = (bf16[4,2,48,128]{3,2,1,0:T(8,128)(2,1)S(1)}, bf16[4,2,48,128]{3,2,1,0:T(8,128)(2,1)S(1)}, u32[]{:S(2)}, u32[]{:S(2)}) collective-permute-start(bf16[4,2,48,128]{3,2,1,0:T(8,128)(2,1)S(1)} %pad_maximum_fusion.3), channel_id=1, source_target_pairs={{0,2},{2,0},{1,3},{3,1},{4,6},{6,4},{5,7},{7,5},{8,10},{10,8},{9,1... | collective-permute-start | bytes 294920 | tf_op jit(solution)/shard_map/ppermute | solution.py:468
  102.3 23.4 %collective-permute-start.8 = (bf16[576,128]{1,0:T(8,128)(2,1)S(1)}, bf16[576,128]{1,0:T(8,128)(2,1)S(1)}, u32[]{:S(2)}, u32[]{:S(2)}) collective-permute-start(bf16[576,128]{1,0:T(8,128)(2,1)S(1)} %reduce_sum.22), channel_id=1, source_target_pairs={{0,2},{2,0},{1,3},{3,1},{4,6},{6,4},{5,7},{7,5},{8,10},{10,8},{9,1... | collective-permute-start | bytes 442376 | tf_op jit(solution)/shard_map/ppermute | solution.py:471
  111.9 0.6 copy-start.8
  114.9 14.9 %all-to-all-start.1 = ((bf16[4,768,128]{2,1,0:T(8,128)(2,1)}), bf16[4,768,128]{2,1,0:T(8,128)(2,1)S(1)}, u32[]{:S(2)}, u32[]{:S(2)}) async-start(bf16[4,768,128]{2,1,0:T(8,128)(2,1)} %shard_map.96), calls=%async_computation.1 | async-start | bytes 1572864 | tf_op jit(solution)/shard_map/all_to_all | solution.py:473
  125.7 0.7 copy-start.7
  127.9 2.0 %copy-start.3 = (bf16[64,128]{1,0:T(8,128)(2,1)S(1)}, bf16[64,128]{1,0:T(8,128)(2,1)}, u32[]{:S(2)}) copy-start(bf16[64,128]{1,0:T(8,128)(2,1)} %get-tuple-element.34) | copy-start | bytes 49156
  127.9 2.6 %copy-start.2 = (bf16[128,512]{1,0:T(8,128)(2,1)S(1)}, bf16[128,512]{1,0:T(8,128)(2,1)}, u32[]{:S(2)}) copy-start(bf16[128,512]{1,0:T(8,128)(2,1)} %get-tuple-element.33) | copy-start | bytes 393220
